TPU v7x, 32 devices: a whole 2x2x4 slice. The times are simulated.
32 devices in a mesh: cfg: 2 (over core), tok: 16 (over z, y, x).
Axes of the slice: x: 2, y: 2, z: 4, core: 2. Of those that a mesh axis runs over, the one named last changes fastest.
Arguments:
- hidden_in: bfloat16 [3072, 1152], P('tok'), may hold values from -6 to 6
- noisy_latent: float32 [3072, 16], P('tok'), may hold values from -6 to 6
- piece_rows: int32 [2, 8], replicated, may hold values from 1 to 192, 1024 in all within a row
- modulation: float32 [2, 2, 8, 1152], P('cfg'), may hold values from -3 to 3
- qkv_weight: bfloat16 [16, 1152, 432], P('tok'), may hold values from -1 to 1, as said below
- proj_weight: bfloat16 [16, 1152, 144], P('tok'), may hold values from -1 to 1, as said below
- up_weight: bfloat16 [16, 1152, 576], P('tok'), may hold values from -1 to 1, as said below
- down_weight: bfloat16 [16, 1152, 576], P('tok'), may hold values from -1 to 1, as said below
- final_weight: bfloat16 [1152, 16], replicated, may hold values from -0.1875 to 0.1875
- guidance: float32 [2], replicated, may hold values from 1.5 to 4.5
- solver_coef: float32 [2, 2], replicated, may hold values from 0.3 to 1.2
Outputs:
- next_latent: float32 [3072, 16], P('tok')
- block_out: bfloat16 [2, 3072, 1152], P('cfg', 'tok')
Inputs may be any that keep to these rules, and one draw needn't show every extreme that they name: Row l of piece_rows sums to 1024; in every row the largest entry is 192. `qkv_weight`: copy i equals copy i % 8. `proj_weight`: copy i equals copy i % 8. `up_weight`: copy i equals copy i % 8. `down_weight`: copy i equals copy i % 8.
All inputs are finite; a program needn't handle non-finite values.
Results may differ from a plain program's by a relative error of at most 0.008.
Values may be sent and summed in bfloat16 or wider, within the bound.
No kernel may reach another device: no remote copies, remote signals or barrier semaphores. Data moves between devices by JAX's collectives and lax.ppermute only.
A program may use at most 64 MiB of HBM per device.

v0:
```python
import functools
import math

import jax
import jax.numpy as jnp
from jax import lax
from jax.experimental import pallas as pl
from jax.experimental.pallas import tpu as pltpu
from jax.sharding import PartitionSpec as P

HEAD_DIM = 72
GROUP = 8
LEN = 1024
LANES = 128
ALIGN = 16
LARGE = ((1, 2, 4), (2, 4, 1))
SMALL = (4, 1, 2)
PROJ = ((2, 4, 1), (4, 1, 2))
HEADS_TO = ((2, 4, 1), (4, 1, 2))
FAR_EARLY = (64, 240, 160)
F32 = jnp.float32
BF16 = jnp.bfloat16


def permute_by(block, offsets):
    count = lax.axis_size("tok")
    route = [
        (half * count + i, half * count + (i ^ offset))
        for half, offset in enumerate(offsets)
        for i in range(count)
    ]
    return lax.ppermute(block, ("cfg", "tok"), route)


def from_other_half(block):
    return lax.ppermute(block, "cfg", [(0, 1), (1, 0)])


def after(value, *earlier):
    return lax.optimization_barrier((value,) + earlier)[0]


def place():
    pos = lax.axis_index("tok")
    return lax.axis_index("cfg"), pos // GROUP, pos % GROUP


def normalized(values):
    center = values - jnp.mean(values, axis=-1, keepdims=True)
    spread = jnp.mean(center * center, axis=-1, keepdims=True)
    return center * lax.rsqrt(spread + 1e-06)


def mod_row(mod_ref, latent, k):
    return mod_ref[latent, k : k + 1, :]


def call(kernel, out_shape, operands, scratch=(), specs=None, flops=0, name=None, vmem=40):
    whole = pl.BlockSpec(memory_space=pltpu.VMEM)
    moved = sum(math.prod(o.shape) * o.dtype.itemsize for o in operands)
    return pl.pallas_call(
        kernel,
        out_shape=out_shape,
        in_specs=specs or [whole] * len(operands),
        out_specs=jax.tree.map(lambda _: whole, out_shape),
        scratch_shapes=list(scratch),
        compiler_params=pltpu.CompilerParams(vmem_limit_bytes=vmem << 20),
        cost_estimate=pl.CostEstimate(flops=flops, bytes_accessed=moved, transcendentals=0),
        name=name,
    )(*operands)


def qkv_kernel(row_counts, mod_ref, weight_ref, *refs):
    row_refs, out_ref, normed, padded = refs[:-3], refs[-3], refs[-2], refs[-1]
    _, latent, _ = place()
    shift, scale = mod_row(mod_ref, latent, 0), 1.0 + mod_row(mod_ref, latent, 1)
    chunk = 32
    at = 0
    for ref, count in zip(row_refs, row_counts):
        for low in range(0, count, chunk):
            rows = ref[low : low + chunk, :].astype(F32)
            normed[at : at + chunk, :] = (normalized(rows) * scale + shift).astype(BF16)
            at += chunk
    weight = weight_ref[...].astype(F32)
    unused = jnp.zeros((LANES - HEAD_DIM, weight.shape[1]), F32)
    for part in range(weight.shape[0] // HEAD_DIM):
        rows = jnp.concatenate([weight[part * HEAD_DIM : (part + 1) * HEAD_DIM], unused])
        padded[part * LANES : (part + 1) * LANES, :] = rows.astype(BF16)
    lane = lax.broadcasted_iota(jnp.int32, (1, padded.shape[0]), 1)
    width = padded.shape[0] // 3
    factor = jnp.where(lane < width, HEAD_DIM ** (-0.5) * math.log2(math.e), 1.0)
    ones = jnp.where((lane >= 2 * width) & (lane % LANES == HEAD_DIM), 1.0, 0.0)
    block = at // 2
    for low in range(0, at, block):
        out = lax.dot_general(
            normed[low : low + block, :], padded[...], (((1,), (1,)), ((), ())), preferred_element_type=F32
        )
        out_ref[low : low + block, :] = (out * factor + ones).astype(BF16)


def qkv_rows(modulation, weight, pieces, row_counts, name):
    count = sum(row_counts)
    parts, width = weight.shape[0] // HEAD_DIM, weight.shape[1]
    return call(
        functools.partial(qkv_kernel, row_counts),
        jax.ShapeDtypeStruct((count, parts * LANES), BF16),
        (modulation, weight) + tuple(pieces),
        scratch=[pltpu.VMEM((count, width), BF16), pltpu.VMEM((parts * LANES, width), BF16)],
        flops=2 * count * width * parts * LANES,
        name=name,
    )


def position(order, offset):
    return sum(1 << i for i, bit in enumerate(order) if offset & bit)


def spread(order, index):
    return sum(bit for i, bit in enumerate(order) if index >> i & 1)


def attention_kernel(cap, packed_rows, counts_ref, early_ref, late_ref, near_ref, far_ref, packed, out):
    core, latent, member = place()
    half = cap // 2
    large, small = 2 * half // 3, half // 3
    width = early_ref.shape[1] // 3
    heads = width // LANES
    counts = [counts_ref[latent, member ^ d] for d in range(GROUP)]
    starts = [jnp.int32(0)]
    for d in range(GROUP):
        starts.append(starts[-1] + (counts[d] + ALIGN - 1) // ALIGN * ALIGN)
    total_rows = packed.shape[0]
    spare = total_rows - LEN
    packed[LEN:, :] = jnp.zeros((spare, packed.shape[1]), BF16)
    for d in range(GROUP):
        for k in range(2):
            away = (core != k).astype(jnp.int32)
            for is_small in range(2):
                size = small if is_small else large
                first = k * half + is_small * large
                where = position(SMALL if is_small else LARGE[k], d)
                if where == 0:
                    rows = early_ref[first : first + size, :]
                elif where < 4:
                    base = cap + is_small * 3 * large + (where - 1) * size
                    base = pl.multiple_of(base + away * (3 * half), 32)
                    rows = early_ref[pl.ds(base, size), :]
                else:
                    base = is_small * 4 * large + (where - 4) * size
                    base = pl.multiple_of(base + away * (4 * half), 32)
                    rows = late_ref[pl.ds(base, size), :]
                packed[pl.ds(pl.multiple_of(starts[d] + first, ALIGN), size), :] = rows
    slot = lax.broadcasted_iota(jnp.int32, (1, packed_rows), 1)
    valid = jnp.zeros((1, packed_rows), jnp.bool_)
    for d in range(GROUP):
        valid = valid | ((slot >= starts[d]) & (slot < starts[d] + counts[d]))
    bias = jnp.where(valid, 0.0, -1e30)
    out[LEN:, :] = jnp.zeros((spare, out.shape[1]), F32)
    block = packed_rows // 3
    for low in range(0, packed_rows, block):
        for head in range(heads):
            lanes = head * LANES
            queries = packed[low : low + block, lanes : lanes + LANES]
            keys = packed[:packed_rows, width + lanes : width + lanes + LANES]
            values = packed[:packed_rows, 2 * width + lanes : 2 * width + lanes + LANES]
            scores = lax.dot_general(
                queries, keys, (((1,), (1,)), ((), ())), preferred_element_type=F32
            )
            scores = scores + bias
            peak = jnp.max(scores, axis=-1, keepdims=True)
            probs = jnp.exp2(scores - peak).astype(BF16)
            mixed = jnp.dot(probs, values, preferred_element_type=F32)
            mixed = mixed / mixed[:, HEAD_DIM : HEAD_DIM + 1]
            out[low : low + block, lanes : lanes + LANES] = mixed
    targets = [
        jnp.where(core == 0, starts[spread(HEADS_TO[0], j)], starts[spread(HEADS_TO[1], j)])
        for j in range(GROUP)
    ]
    for pair in range(0, GROUP, 2):
        columns = []
        for head in range(heads):
            rows = [
                out[pl.ds(pl.multiple_of(targets[j], ALIGN), cap), head * LANES : (head + 1) * LANES]
                for j in (pair, pair + 1)
            ]
            columns.append(jnp.concatenate(rows).T[:HEAD_DIM])
        dest = near_ref if pair < GROUP // 2 else far_ref
        at = pair % (GROUP // 2) * cap
        dest[:, at : at + 2 * cap] = jnp.concatenate(columns).astype(BF16)


def attention(piece_rows, early, late, cap):
    packed_rows = LEN + GROUP * ALIGN
    total = -(-(packed_rows + cap) // 32) * 32
    width = early.shape[1] // 3
    heads = width // LANES
    shape = jax.ShapeDtypeStruct((heads * HEAD_DIM, GROUP // 2 * cap), BF16)
    return call(
        functools.partial(attention_kernel, cap, packed_rows),
        (shape, shape),
        (piece_rows, early, late),
        scratch=[pltpu.VMEM((total, 3 * width), BF16), pltpu.VMEM((total, width), F32)],
        specs=[pl.BlockSpec(memory_space=pltpu.SMEM)] + [pl.BlockSpec(memory_space=pltpu.VMEM)] * 2,
        flops=4 * heads * packed_rows * packed_rows * LANES,
        name="attend",
    )


def project_kernel(cap, mod_ref, hidden_ref, mine_ref, mate_ref, *refs):
    proj_refs, plane_refs = refs[:8], refs[8 : 8 + GROUP // 2 - 1]
    mid_ref, mlp_ref, flat, weights = refs[8 + GROUP // 2 - 1 :]
    core, latent, member = place()
    heads = mine_ref.shape[0] // HEAD_DIM

    def put(block, j):
        offset = jnp.where(core == 0, spread(HEADS_TO[0], j), spread(HEADS_TO[1], j))
        for head in range(heads):
            rows = block[head * HEAD_DIM : (head + 1) * HEAD_DIM]
            flat[head * GROUP + offset] = rows

    put(mine_ref[...][:, :cap].astype(F32), 0)
    put(mate_ref[...][:, :cap].astype(F32), GROUP // 2)
    for j, ref in enumerate(plane_refs):
        both = ref[...].astype(F32)
        put(both[:, :cap], j + 1)
        put(both[:, cap:], (j + 1) ^ (GROUP // 2))
    for away in range(2):
        head = core if away == 0 else 1 - core
        at = 0
        for blocks, ref in zip((1, 1, 2, 4), proj_refs[4 * away : 4 * away + 4]):
            block = ref[ref.shape[0] - blocks * HEAD_DIM :, :].astype(F32)
            for row in range(0, block.shape[0], HEAD_DIM):
                offset = jnp.where(head == 0, spread(PROJ[0], at), spread(PROJ[1], at))
                weights[head * GROUP + offset] = block[row : row + HEAD_DIM]
                at += 1
    stacked = flat[...].reshape(heads * GROUP * HEAD_DIM, cap).astype(BF16)
    proj = weights[...].reshape(heads * GROUP * HEAD_DIM, weights.shape[2]).astype(BF16)
    attn_out = lax.dot_general(stacked, proj, (((0,), (0,)), ((), ())), preferred_element_type=F32)
    mid = hidden_ref[...].astype(F32) + mod_row(mod_ref, latent, 2) * attn_out
    mid_ref[...] = mid
    scale, shift = 1.0 + mod_row(mod_ref, latent, 4), mod_row(mod_ref, latent, 3)
    mlp_ref[...] = (normalized(mid) * scale + shift).astype(BF16)


def project(modulation, hidden_in, proj_parts, mine, mate, plane):
    cap, width = hidden_in.shape
    heads = mine.shape[0] // HEAD_DIM
    return call(
        functools.partial(project_kernel, cap),
        (jax.ShapeDtypeStruct((cap, width), F32), jax.ShapeDtypeStruct((cap, width), BF16)),
        (modulation, hidden_in, mine, mate) + tuple(proj_parts) + tuple(plane),
        scratch=[
            pltpu.VMEM((heads * GROUP, HEAD_DIM, cap), F32),
            pltpu.VMEM((heads * GROUP, HEAD_DIM, width), F32),
        ],
        flops=2 * cap * width * width,
        name="project",
    )


def pack_kernel(up_ref, down_ref, *refs):
    far_refs, (up_all, down_all, sems) = refs[:-3], refs[-3:]
    core, _, _ = place()
    hidden, parts = up_ref.shape[0], len(far_refs) // 2
    own = [
        pltpu.make_async_copy(up_ref, up_all.at[pl.ds(0, hidden)], sems.at[2 * parts]),
        pltpu.make_async_copy(down_ref, down_all.at[pl.ds(0, hidden)], sems.at[2 * parts + 1]),
    ]
    for copy in own:
        copy.start()

    def fetch(dests):
        copies = []
        for d, dest in enumerate(dests):
            at = hidden
            for ref in far_refs[parts * d : parts * (d + 1)]:
                rows = ref.shape[0]
                copies.append(
                    pltpu.make_async_copy(ref, dest.at[pl.ds(at, rows)], sems.at[len(copies)])
                )
                at += rows
        for copy in copies:
            copy.start()
        for copy in copies:
            copy.wait()

    pl.when(core == 0)(lambda: fetch((up_all, down_all)))
    pl.when(core == 1)(lambda: fetch((down_all, up_all)))
    for copy in own:
        copy.wait()


def pack(up, down, far):
    hidden, width = up.shape
    both = jax.ShapeDtypeStruct((2 * hidden, width), BF16)
    return call(
        pack_kernel,
        (both, both),
        (up, down) + tuple(far),
        scratch=[pltpu.SemaphoreType.DMA((2 + len(far),))],
        specs=[pl.BlockSpec(memory_space=pl.ANY)] * (2 + len(far)),
        name="pack",
    )


def mlp_kernel(row_count, out_count, up_ref, down_ref, *refs):
    row_refs, out_refs, rows = refs[:row_count], refs[row_count:-1], refs[-1]
    at = 0
    for ref in row_refs:
        rows[at : at + ref.shape[0], :] = ref[...]
        at += ref.shape[0]
    units = lax.dot_general(
        rows[...], up_ref[...], (((1,), (1,)), ((), ())), preferred_element_type=F32
    )
    units = 0.5 * units * (1.0 + jnp.tanh(0.7978845608 * (units + 0.044715 * (units * units * units))))
    partial = jnp.dot(units.astype(BF16), down_ref[...], preferred_element_type=F32)
    at = 0
    for ref in out_refs:
        ref[...] = partial[at : at + ref.shape[0]].astype(ref.dtype)
        at += ref.shape[0]


def mlp_rows(pieces, packed, out_rows, dtype, name):
    count = sum(p.shape[0] for p in pieces)
    hidden, width = packed[0].shape
    outs = tuple(jax.ShapeDtypeStruct((rows, width), dtype) for rows in out_rows)
    return call(
        functools.partial(mlp_kernel, len(pieces), len(outs)),
        outs,
        tuple(packed) + tuple(pieces),
        scratch=[pltpu.VMEM((count, width), BF16)],
        flops=4 * count * width * hidden,
        name=name,
    )


def final_kernel(
    counts_ref, guide_ref, coef_ref, mod_ref, mid_ref, part_ref, noisy_ref, weight_ref,
    first_low, first_high, second_low, second_high, block_ref, pred_ref, base_ref, total,
):
    core, latent, member = place()
    cap = mid_ref.shape[0]
    half = cap // 2
    for low, first, second in ((0, first_low, second_low), (half, first_high, second_high)):
        total[low : low + half, :] = (
            part_ref[low : low + half, :] + first[:half, :].astype(F32) + second[...].astype(F32)
        )
    rows = (mid_ref[...] + mod_row(mod_ref, latent, 5) * total[...]).astype(BF16).astype(F32)
    count = counts_ref[latent, member]
    rows = jnp.where(lax.broadcasted_iota(jnp.int32, (cap, 1), 0) < count, rows, 0.0)
    block_ref[...] = rows.astype(BF16)
    scale, shift = 1.0 + mod_row(mod_ref, latent, 7), mod_row(mod_ref, latent, 6)
    final_in = (normalized(rows) * scale + shift).astype(BF16)
    pred = lax.dot_general(
        weight_ref[...], final_in, (((1,), (1,)), ((), ())), preferred_element_type=F32
    )
    guide = guide_ref[latent]
    valid = lax.broadcasted_iota(jnp.int32, (1, cap), 1) < count
    weighted = (-coef_ref[latent, 1] * jnp.where(core == 0, guide, 1.0 - guide)) * pred
    pred_ref[...] = jnp.where(valid, weighted, 0.0)
    base_ref[...] = jnp.where(valid, coef_ref[latent, 0] * noisy_ref[...], 0.0)


def final(scalars, modulation, mid, part, noisy, weight, firsts, seconds):
    cap, width = mid.shape
    smem, vmem = pl.BlockSpec(memory_space=pltpu.SMEM), pl.BlockSpec(memory_space=pltpu.VMEM)
    flat = jax.ShapeDtypeStruct(noisy.shape, F32)
    return call(
        final_kernel,
        (jax.ShapeDtypeStruct((cap, width), BF16), flat, flat),
        tuple(scalars) + (modulation, mid, part, noisy, weight) + tuple(firsts) + tuple(seconds),
        scratch=[pltpu.VMEM((cap, width), F32)],
        specs=[smem] * 3 + [vmem] * 9,
        flops=2 * cap * width * weight.shape[0],
        name="finish",
    )


def shards(
    hidden_in,
    noisy_latent,
    piece_rows,
    modulation,
    qkv_weight,
    proj_weight,
    up_weight,
    down_weight,
    final_weight,
    guidance,
    solver_coef,
):
    cap, width = hidden_in.shape
    half = cap // 2
    large, small = 2 * half // 3, half // 3
    core, _, _ = place()
    modulation = modulation[0]
    qkv_rows_t, proj_t, up_t, down_t = (
        w[0].T for w in (qkv_weight, proj_weight, up_weight, down_weight)
    )

    own_rows = after(lax.dynamic_slice_in_dim(hidden_in, core * half, half))
    large_rows, small_rows = own_rows[:large], own_rows[large:]
    hidden = up_t.shape[0]
    cuts = [sum(FAR_EARLY[:i]) for i in range(len(FAR_EARLY) + 1)] + [hidden]
    proj_rows = None
    got, away = [], []
    for step in range(3):
        payload = large_rows if step == 0 else jnp.concatenate([large_rows, proj_rows])
        got_large = permute_by(payload, [order[step] for order in LARGE])
        got_small = permute_by(small_rows, [SMALL[step]] * 2)
        if step == 0:
            up_t, down_t, _ = lax.optimization_barrier((up_t, down_t, got_large))
            sent = [
                jnp.where(core == 0, up_t[low:high], down_t[low:high])
                for low, high in zip(cuts[:-1], cuts[1:])
            ]
            proj_own = [
                lax.dynamic_slice_in_dim(proj_t, head * HEAD_DIM, HEAD_DIM) for head in (core, 1 - core)
            ]
            proj_rows = proj_own[0]
        elif step == 1:
            got_large, got_small = lax.optimization_barrier((got_large, got_small))
            proj_rows = jnp.concatenate([proj_rows, got_large[2 * large :]])
        else:
            early = qkv_rows(
                modulation,
                qkv_rows_t,
                (hidden_in, got[0][0], got[1][0], got[0][1], got[1][1])
                + (away[0][0], away[1][0], away[0][1], away[1][1]),
                (cap, large, 2 * large, small, 2 * small) + (large, 2 * large, small, 2 * small),
                "qkv_early",
            )
            got_large, got_small, early, *sent = lax.optimization_barrier(
                (got_large, got_small, early, *sent)
            )
            proj_rows = jnp.concatenate([proj_rows, got_large[4 * large :]])
        if step < 2:
            large_rows = jnp.concatenate([large_rows, got_large[: large << step]])
            small_rows = jnp.concatenate([small_rows, got_small])
        got.append((got_large, got_small))
        away.append((from_other_half(got_large), from_other_half(got_small)))
    proj_last = permute_by(proj_rows, [order[2] for order in PROJ])
    far = [permute_by(sent[0], [GROUP // 2] * 2)]
    late = qkv_rows(
        modulation,
        qkv_rows_t,
        got[2] + away[2],
        (4 * large, 4 * small) * 2,
        "qkv_late",
    )
    far.append(permute_by(after(sent[1], far[0], late), [GROUP // 2] * 2))
    far.append(permute_by(after(sent[2], far[0], late), [GROUP // 2] * 2))
    mine, sent_heads = attention(piece_rows, early, late, cap)
    mate = permute_by(sent_heads, [order[2] for order in HEADS_TO])
    mate, far[1], proj_last = lax.optimization_barrier((mate, far[1], proj_last))
    proj_parts = [proj_own[0], got[1][0], got[2][0], proj_last]
    proj_parts += [proj_own[1], away[1][0], away[2][0], from_other_half(proj_last)]
    plane = []
    for j in range(1, GROUP // 2):
        both = jnp.concatenate([a[:, j * cap : (j + 1) * cap] for a in (mine, mate)], axis=1)
        plane.append(permute_by(both, [spread(order, j) for order in HEADS_TO]))
    far[2], *plane = lax.optimization_barrier((far[2], *plane))
    far.append(permute_by(after(sent[3], *plane), [GROUP // 2] * 2))
    mid, mlp_in = project(modulation, hidden_in, proj_parts, mine, mate, plane)

    side = permute_by(mlp_in, (1, 2))
    both = [
        jnp.concatenate([rows[low : low + half] for rows in (mlp_in, side)]) for low in (0, half)
    ]
    across = [permute_by(rows, (2, 1)) for rows in both]
    far[3] = after(far[3], *both)
    far += [from_other_half(rows) for rows in far]
    packed = pack(up_t, down_t, far)
    sums = [
        mlp_rows((rows,), packed, (cap,), BF16, f"mlp_far{i}")[0] for i, rows in enumerate(across)
    ]
    firsts = [permute_by(rows, (2, 1)) for rows in sums]
    part, *side_parts = mlp_rows(
        (after(mlp_in, *sums), side), packed, (cap, half, half), F32, "mlp_near"
    )
    seconds = [
        permute_by((rows + first[half:].astype(F32)).astype(BF16), (1, 2))
        for rows, first in zip(side_parts, firsts)
    ]
    block_rows, pred, base = final(
        (piece_rows, guidance, solver_coef),
        modulation,
        mid,
        part,
        noisy_latent.T,
        final_weight.T,
        firsts,
        seconds,
    )
    next_latent = base + (pred + from_other_half(pred))
    return (next_latent.T, block_rows[None])


def solution(mesh):
    placed = (
        P("tok", None),
        P("tok", None),
        P(),
        P("cfg", None, None, None),
        P("tok", None, None),
        P("tok", None, None),
        P("tok", None, None),
        P("tok", None, None),
        P(),
        P(),
        P(),
    )
    return jax.shard_map(
        shards,
        mesh=mesh,
        in_specs=placed,
        out_specs=(P("tok", None), P("cfg", "tok", None)),
        check_vma=False,
    )
```

profile of v0, /device:TPU:0, one launch (start us, length us, event | category | flops | bytes accessed | tf_op | source)
XLA Modules:
  0.0 115.2 jit_solution(18154938667699507787)
XLA Ops:
  1.7 3.1 %collective-permute-start.2 = (bf16[32,1152]{1,0:T(8,128)(2,1)S(1)}, bf16[32,1152]{1,0:T(8,128)(2,1)S(1)}, u32[]{:S(2)}, u32[]{:S(2)}) collective-permute-start(bf16[32,1152]{1,0:T(8,128)(2,1)S(1)} %slice.101), channel_id=1, source_target_pairs={{0,4},{1,5},{2,6},{3,7},{4,0},{5,1},{6,2},{7,3},{8,12},{9,13},{10,... | collective-permute-start | bytes 221192 | tf_op jit(solution)/shard_map/ppermute | solution.py:32
  9.2 2.1 %collective-permute-done.refs_1_ = bf16[64,1152]{1,0:T(8,128)(2,1)S(1)} collective-permute-done((bf16[64,1152]{1,0:T(8,128)(2,1)S(1)}, bf16[64,1152]{1,0:T(8,128)(2,1)S(1)}, u32[]{:S(2)}, u32[]{:S(2)}) %collective-permute-start) | collective-permute-done | bytes 147488 | tf_op jit(solution)/shard_map/ppermute | solution.py:32
  11.3 2.5 %collective-permute-start.1 = (bf16[200,1152]{1,0:T(8,128)(2,1)S(1)}, bf16[200,1152]{1,0:T(8,128)(2,1)S(1)}, u32[]{:S(2)}, u32[]{:S(2)}) collective-permute-start(bf16[200,1152]{1,0:T(8,128)(2,1)S(1)} %pad_maximum_fusion.1), channel_id=1, source_target_pairs={{0,2},{1,3},{2,0},{3,1},{4,6},{5,7},{6,4},{7,5},{8,10},{9,11},{10,... | collective-permute-start | bytes 1382408 | tf_op jit(solution)/shard_map/ppermute | solution.py:32
  14.0 6.3 %collective-permute-done.1.refs_2_.refs_1_ = bf16[200,1152]{1,0:T(8,128)(2,1)S(1)} collective-permute-done((bf16[200,1152]{1,0:T(8,128)(2,1)S(1)}, bf16[200,1152]{1,0:T(8,128)(2,1)S(1)}, u32[]{:S(2)}, u32[]{:S(2)}) %collective-permute-start.1) | collective-permute-done | bytes 460832 | tf_op jit(solution)/shard_map/ppermute | solution.py:32
  21.2 2.1 %collective-permute-start.5 = (bf16[128,1152]{1,0:T(8,128)(2,1)S(1)}, bf16[128,1152]{1,0:T(8,128)(2,1)S(1)}, u32[]{:S(2)}, u32[]{:S(2)}) collective-permute-start(bf16[128,1152]{1,0:T(8,128)(2,1)S(1)} %pad_maximum_fusion.4), channel_id=1, source_target_pairs={{0,2},{1,3},{2,0},{3,1},{4,6},{5,7},{6,4},{7,5},{8,10},{9,11},{10,... | collective-permute-start | bytes 884744 | tf_op jit(solution)/shard_map/ppermute | solution.py:32
  23.4 2.5 %qkv_early.1.early_ref = bf16[768,768]{1,0:T(8,128)(2,1)S(1)} custom-call(f32[2,8,1152]{2,1,0:T(8,128)S(1)} %bitcast.33, bf16[432,1152]{1,0:T(8,128)(2,1)S(1)} %bitcast.39, bf16[192,1152]{1,0:T(8,128)(2,1)S(1)} %copy-done.2, bf16[64,1152]{1,0:T(8,128)(2,1)S(1)} %collective-permute-done.refs_1_, bf16[200,1152]{1,0:T(8,128)(2,1)S(1)} %collective-permute-done.1.refs_2_.refs_1_, ...), custom_call_target="tpu_custom_call" | custom-call | flops 1358954496 | bytes 3170304 | tf_op jit(solution)/shard_map/qkv_early/pallas_call | solution.py:61
  25.9 5.0 %collective-permute-done.5.refs_1_ = bf16[128,1152]{1,0:T(8,128)(2,1)S(1)} collective-permute-done((bf16[128,1152]{1,0:T(8,128)(2,1)S(1)}, bf16[128,1152]{1,0:T(8,128)(2,1)S(1)}, u32[]{:S(2)}, u32[]{:S(2)}) %collective-permute-start.5) | collective-permute-done | bytes 294944 | tf_op jit(solution)/shard_map/ppermute | solution.py:32
  30.9 3.0 %collective-permute-done.4.refs_0_.refs_2_ = bf16[400,1152]{1,0:T(8,128)(2,1)S(1)} collective-permute-done((bf16[400,1152]{1,0:T(8,128)(2,1)S(1)}, bf16[400,1152]{1,0:T(8,128)(2,1)S(1)}, u32[]{:S(2)}, u32[]{:S(2)}) %collective-permute-start.4) | collective-permute-done | bytes 921632 | tf_op jit(solution)/shard_map/ppermute | solution.py:32
  36.8 2.4 %qkv_late.1.late_ref = bf16[768,768]{1,0:T(8,128)(2,1)S(1)} custom-call(f32[2,8,1152]{2,1,0:T(8,128)S(1)} %bitcast.34, bf16[432,1152]{1,0:T(8,128)(2,1)S(1)} %bitcast.40, bf16[400,1152]{1,0:T(8,128)(2,1)S(1)} %collective-permute-done.4.refs_0_.refs_2_, bf16[128,1152]{1,0:T(8,128)(2,1)S(1)} %collective-permute-done.5.refs_1_, ...), custom_call_target="tpu_custom_call" | custom-call | flops 1358954496 | bytes 3502080 | tf_op jit(solution)/shard_map/qkv_late/pallas_call | solution.py:61
  40.7 6.0 %attend.1 = (bf16[144,768]{1,0:T(8,128)(2,1)S(1)}, bf16[144,768]{1,0:T(8,128)(2,1)S(1)}) custom-call(s32[2,8]{1,0:T(2,128)S(1)} %copy-done.6, bf16[768,768]{1,0:T(8,128)(2,1)S(1)} %qkv_early.1.early_ref, bf16[768,768]{1,0:T(8,128)(2,1)S(1)} %qkv_late.1.late_ref), custom_call_target="tpu_custom_call" | custom-call | flops 1358954496 | bytes 2359360 | tf_op jit(solution)/shard_map/attend/pallas_call | solution.py:61
  50.0 2.7 %collective-permute-done.12.mate_ref = bf16[144,768]{1,0:T(8,128)(2,1)S(1)} collective-permute-done((bf16[144,768]{1,0:T(8,128)(2,1)S(1)}, bf16[144,768]{1,0:T(8,128)(2,1)S(1)}, u32[]{:S(2)}, u32[]{:S(2)}) %collective-permute-start.12) | collective-permute-done | bytes 221216 | tf_op jit(solution)/shard_map/ppermute | solution.py:32
  52.7 3.0 %collective-permute-done.14.refs_1_ = bf16[240,1152]{1,0:T(8,128)(2,1)S(1)} collective-permute-done((bf16[240,1152]{1,0:T(8,128)(2,1)S(1)}, bf16[240,1152]{1,0:T(8,128)(2,1)S(1)}, u32[]{:S(2)}, u32[]{:S(2)}) %collective-permute-start.14) | collective-permute-done | bytes 552992 | tf_op jit(solution)/shard_map/ppermute | solution.py:32
  56.0 2.1 %collective-permute-start.18 = (bf16[144,384]{1,0:T(8,128)(2,1)S(1)}, bf16[144,384]{1,0:T(8,128)(2,1)S(1)}, u32[]{:S(2)}, u32[]{:S(2)}) collective-permute-start(bf16[144,384]{1,0:T(8,128)(2,1)S(1)} %pad_maximum_fusion.6), channel_id=1, source_target_pairs={{0,2},{1,3},{2,0},{3,1},{4,6},{5,7},{6,4},{7,5},{8,10},{9,11},{10,... | collective-permute-start | bytes 331784 | tf_op jit(solution)/shard_map/ppermute | solution.py:32
  59.9 3.8 %collective-permute-done.17.refs_2_ = bf16[160,1152]{1,0:T(8,128)(2,1)S(1)} collective-permute-done((bf16[160,1152]{1,0:T(8,128)(2,1)S(1)}, bf16[160,1152]{1,0:T(8,128)(2,1)S(1)}, u32[]{:S(2)}, u32[]{:S(2)}) %collective-permute-start.17) | collective-permute-done | bytes 368672 | tf_op jit(solution)/shard_map/ppermute | solution.py:32
  65.4 2.6 %collective-permute-done.20.refs_10_ = bf16[144,384]{1,0:T(8,128)(2,1)S(1)} collective-permute-done((bf16[144,384]{1,0:T(8,128)(2,1)S(1)}, bf16[144,384]{1,0:T(8,128)(2,1)S(1)}, u32[]{:S(2)}, u32[]{:S(2)}) %collective-permute-start.20) | collective-permute-done | bytes 110624 | tf_op jit(solution)/shard_map/ppermute | solution.py:32
  68.6 1.9 %project.1 = (f32[192,1152]{1,0:T(8,128)S(1)}, bf16[192,1152]{1,0:T(8,128)(2,1)S(1)}) custom-call(f32[2,8,1152]{2,1,0:T(8,128)S(1)} %bitcast.35, bf16[192,1152]{1,0:T(8,128)(2,1)S(1)} %copy-done.2, bf16[144,768]{1,0:T(8,128)(2,1)S(1)} %get-tuple-element.44.mine_ref, bf16[144,768]{1,0:T(8,128)(2,1)S(1)} %collective-permute-done.12.mate_ref, ...), custom_call_target="tpu_custom_call" | custom-call | flops 509607936 | bytes 5713920 | tf_op jit(solution)/shard_map/project/pallas_call | solution.py:61
  72.1 6.8 %collective-permute-done.22.refs_1_ = bf16[192,1152]{1,0:T(8,128)(2,1)S(1)} collective-permute-done((bf16[192,1152]{1,0:T(8,128)(2,1)S(1)}, bf16[192,1152]{1,0:T(8,128)(2,1)S(1)}, u32[]{:S(2)}, u32[]{:S(2)}) %collective-permute-start.22) | collective-permute-done | bytes 442400 | tf_op jit(solution)/shard_map/ppermute | solution.py:32
  83.1 4.2 %collective-permute-done.27.refs_0_ = bf16[192,1152]{1,0:T(8,128)(2,1)S(1)} collective-permute-done((bf16[192,1152]{1,0:T(8,128)(2,1)S(1)}, bf16[192,1152]{1,0:T(8,128)(2,1)S(1)}, u32[]{:S(2)}, u32[]{:S(2)}) %collective-permute-start.27) | collective-permute-done | bytes 442400 | tf_op jit(solution)/shard_map/ppermute | solution.py:32
  89.8 2.2 %collective-permute-done.28.refs_0_ = bf16[192,1152]{1,0:T(8,128)(2,1)S(1)} collective-permute-done((bf16[192,1152]{1,0:T(8,128)(2,1)S(1)}, bf16[192,1152]{1,0:T(8,128)(2,1)S(1)}, u32[]{:S(2)}, u32[]{:S(2)}) %collective-permute-start.28) | collective-permute-done | bytes 442400 | tf_op jit(solution)/shard_map/ppermute | solution.py:32
  94.5 2.8 %mlp_near.1 = (f32[192,1152]{1,0:T(8,128)S(1)}, f32[96,1152]{1,0:T(8,128)S(1)}, f32[96,1152]{1,0:T(8,128)S(1)}) custom-call(bf16[1152,1152]{1,0:T(8,128)(2,1)S(1)} %get-tuple-element.63.up_ref, bf16[1152,1152]{1,0:T(8,128)(2,1)S(1)} %get-tuple-element.64.down_ref, bf16[192,1152]{1,0:T(8,128)(2,1)S(1)} %get-tuple-element.65.refs_0_, ...), custom_call_target="tpu_custom_call" | custom-call | flops 2038431744 | bytes 6193152 | tf_op jit(solution)/shard_map/mlp_near/pallas_call | solution.py:61
  99.1 5.8 %collective-permute-done.30.first_high = bf16[192,1152]{1,0:T(8,128)(2,1)S(1)} collective-permute-done((bf16[192,1152]{1,0:T(8,128)(2,1)S(1)}, bf16[192,1152]{1,0:T(8,128)(2,1)S(1)}, u32[]{:S(2)}, u32[]{:S(2)}) %collective-permute-start.30) | collective-permute-done | bytes 442400 | tf_op jit(solution)/shard_map/ppermute | solution.py:32
  105.0 2.6 %collective-permute-start.32 = (bf16[96,1152]{1,0:T(8,128)(2,1)S(1)}, bf16[96,1152]{1,0:T(8,128)(2,1)S(1)}, u32[]{:S(2)}, u32[]{:S(2)}) collective-permute-start(bf16[96,1152]{1,0:T(8,128)(2,1)S(1)} %add_convert_fusion), channel_id=1, source_target_pairs={{0,1},{1,0},{2,3},{3,2},{4,5},{5,4},{6,7},{7,6},{8,9},{9,8},{10,11... | collective-permute-start | bytes 663560 | tf_op jit(solution)/shard_map/ppermute | solution.py:32
  107.5 3.9 %collective-permute-done.32.second_high = bf16[96,1152]{1,0:T(8,128)(2,1)S(1)} collective-permute-done((bf16[96,1152]{1,0:T(8,128)(2,1)S(1)}, bf16[96,1152]{1,0:T(8,128)(2,1)S(1)}, u32[]{:S(2)}, u32[]{:S(2)}) %collective-permute-start.32) | collective-permute-done | bytes 221216 | tf_op jit(solution)/shard_map/ppermute | solution.py:32
  111.4 1.9 %finish.1 = (bf16[192,1152]{1,0:T(8,128)(2,1)}, f32[16,192]{1,0:T(8,128)S(1)}, f32[16,192]{1,0:T(8,128)S(1)}) custom-call(s32[2,8]{1,0:T(2,128)S(1)} %copy-done.6, f32[2]{0:T(128)S(1)} %copy-done.8, f32[2,2]{1,0:T(2,128)S(1)} %copy-done.7, f32[2,8,1152]{2,1,0:T(8,128)S(1)} %bitcast.36, f32[192,1152]{1,0:T(8,128)S(1)} %get-tuple-element.56.mid_ref, ...), custom_call_target="tpu_custom_call" | custom-call | flops 7077888 | bytes 3219544 | tf_op jit(solution)/shard_map/finish/pallas_call | solution.py:61
  (104 shorter events, 32.8 us)
Async XLA Ops:
  1.7 6.3 %collective-permute-start.2 = (bf16[32,1152]{1,0:T(8,128)(2,1)S(1)}, bf16[32,1152]{1,0:T(8,128)(2,1)S(1)}, u32[]{:S(2)}, u32[]{:S(2)}) collective-permute-start(bf16[32,1152]{1,0:T(8,128)(2,1)S(1)} %slice.101), channel_id=1, source_target_pairs={{0,4},{1,5},{2,6},{3,7},{4,0},{5,1},{6,2},{7,3},{8,12},{9,13},{10,... | collective-permute-start | bytes 221192 | tf_op jit(solution)/shard_map/ppermute | solution.py:32
  9.2 12.0 %collective-permute-start.8 = (bf16[32,1152]{1,0:T(8,128)(2,1)S(1)}, bf16[32,1152]{1,0:T(8,128)(2,1)S(1)}, u32[]{:S(2)}, u32[]{:S(2)}) collective-permute-start(bf16[32,1152]{1,0:T(8,128)(2,1)S(1)} %collective-permute-done.2.refs_3_), channel_id=1, source_target_pairs={{0,16},{16,0},{1,17},{17,1},{2,18},{18,2},{3,19},{19,3},{4,20},{20... | collective-permute-start | bytes 221192 | tf_op jit(solution)/shard_map/ppermute | solution.py:36
  11.3 8.9 %collective-permute-start.1 = (bf16[200,1152]{1,0:T(8,128)(2,1)S(1)}, bf16[200,1152]{1,0:T(8,128)(2,1)S(1)}, u32[]{:S(2)}, u32[]{:S(2)}) collective-permute-start(bf16[200,1152]{1,0:T(8,128)(2,1)S(1)} %pad_maximum_fusion.1), channel_id=1, source_target_pairs={{0,2},{1,3},{2,0},{3,1},{4,6},{5,7},{6,4},{7,5},{8,10},{9,11},{10,... | collective-permute-start | bytes 1382408 | tf_op jit(solution)/shard_map/ppermute | solution.py:32
  20.4 13.5 %collective-permute-start.4 = (bf16[400,1152]{1,0:T(8,128)(2,1)S(1)}, bf16[400,1152]{1,0:T(8,128)(2,1)S(1)}, u32[]{:S(2)}, u32[]{:S(2)}) collective-permute-start(bf16[400,1152]{1,0:T(8,128)(2,1)S(1)} %get-tuple-element.73), channel_id=1, source_target_pairs={{0,4},{1,5},{2,6},{3,7},{4,0},{5,1},{6,2},{7,3},{8,12},{9,13},{10,... | collective-permute-start | bytes 2764808 | tf_op jit(solution)/shard_map/ppermute | solution.py:32
  21.2 9.7 %collective-permute-start.5 = (bf16[128,1152]{1,0:T(8,128)(2,1)S(1)}, bf16[128,1152]{1,0:T(8,128)(2,1)S(1)}, u32[]{:S(2)}, u32[]{:S(2)}) collective-permute-start(bf16[128,1152]{1,0:T(8,128)(2,1)S(1)} %pad_maximum_fusion.4), channel_id=1, source_target_pairs={{0,2},{1,3},{2,0},{3,1},{4,6},{5,7},{6,4},{7,5},{8,10},{9,11},{10,... | collective-permute-start | bytes 884744 | tf_op jit(solution)/shard_map/ppermute | solution.py:32
  34.6 15.4 %collective-permute-start.15 = (bf16[288,1152]{1,0:T(8,128)(2,1)S(1)}, bf16[288,1152]{1,0:T(8,128)(2,1)S(1)}, u32[]{:S(2)}, u32[]{:S(2)}) collective-permute-start(bf16[288,1152]{1,0:T(8,128)(2,1)S(1)} %pad_maximum_fusion), channel_id=1, source_target_pairs={{0,1},{1,0},{2,3},{3,2},{4,5},{5,4},{6,7},{7,6},{8,9},{9,8},{10,11... | collective-permute-start | bytes 1990664 | tf_op jit(solution)/shard_map/ppermute | solution.py:32
  40.3 15.5 %collective-permute-start.14 = (bf16[240,1152]{1,0:T(8,128)(2,1)S(1)}, bf16[240,1152]{1,0:T(8,128)(2,1)S(1)}, u32[]{:S(2)}, u32[]{:S(2)}) collective-permute-start(bf16[240,1152]{1,0:T(8,128)(2,1)S(1)} %slice_select_fusion), channel_id=1, source_target_pairs={{0,4},{1,5},{2,6},{3,7},{4,0},{5,1},{6,2},{7,3},{8,12},{9,13},{10,... | collective-permute-start | bytes 1658888 | tf_op jit(solution)/shard_map/ppermute | solution.py:32
  46.7 6.0 %collective-permute-start.12 = (bf16[144,768]{1,0:T(8,128)(2,1)S(1)}, bf16[144,768]{1,0:T(8,128)(2,1)S(1)}, u32[]{:S(2)}, u32[]{:S(2)}) collective-permute-start(bf16[144,768]{1,0:T(8,128)(2,1)S(1)} %get-tuple-element.45), channel_id=1, source_target_pairs={{0,1},{1,0},{2,3},{3,2},{4,5},{5,4},{6,7},{7,6},{8,9},{9,8},{10,11... | collective-permute-start | bytes 663560 | tf_op jit(solution)/shard_map/ppermute | solution.py:32
  48.2 15.5 %collective-permute-start.17 = (bf16[160,1152]{1,0:T(8,128)(2,1)S(1)}, bf16[160,1152]{1,0:T(8,128)(2,1)S(1)}, u32[]{:S(2)}, u32[]{:S(2)}) collective-permute-start(bf16[160,1152]{1,0:T(8,128)(2,1)S(1)} %slice_select_fusion.1), channel_id=1, source_target_pairs={{0,4},{1,5},{2,6},{3,7},{4,0},{5,1},{6,2},{7,3},{8,12},{9,13},{10,... | collective-permute-start | bytes 1105928 | tf_op jit(solution)/shard_map/ppermute | solution.py:32
  55.8 12.8 %collective-permute-start.16 = (bf16[288,1152]{1,0:T(8,128)(2,1)S(1)}, bf16[288,1152]{1,0:T(8,128)(2,1)S(1)}, u32[]{:S(2)}, u32[]{:S(2)}) collective-permute-start(bf16[288,1152]{1,0:T(8,128)(2,1)S(1)} %collective-permute-done.15.refs_3_), channel_id=1, source_target_pairs={{0,16},{16,0},{1,17},{17,1},{2,18},{18,2},{3,19},{19,3},{4,20},{20... | collective-permute-start | bytes 1990664 | tf_op jit(solution)/shard_map/ppermute | solution.py:36
  56.0 7.7 %collective-permute-start.18 = (bf16[144,384]{1,0:T(8,128)(2,1)S(1)}, bf16[144,384]{1,0:T(8,128)(2,1)S(1)}, u32[]{:S(2)}, u32[]{:S(2)}) collective-permute-start(bf16[144,384]{1,0:T(8,128)(2,1)S(1)} %pad_maximum_fusion.6), channel_id=1, source_target_pairs={{0,2},{1,3},{2,0},{3,1},{4,6},{5,7},{6,4},{7,5},{8,10},{9,11},{10,... | collective-permute-start | bytes 331784 | tf_op jit(solution)/shard_map/ppermute | solution.py:32
  58.2 7.2 %collective-permute-start.19 = (bf16[144,384]{1,0:T(8,128)(2,1)S(1)}, bf16[144,384]{1,0:T(8,128)(2,1)S(1)}, u32[]{:S(2)}, u32[]{:S(2)}) collective-permute-start(bf16[144,384]{1,0:T(8,128)(2,1)S(1)} %pad_maximum_fusion.7), channel_id=1, source_target_pairs={{0,4},{1,5},{2,6},{3,7},{4,0},{5,1},{6,2},{7,3},{8,12},{9,13},{10,... | collective-permute-start | bytes 331784 | tf_op jit(solution)/shard_map/ppermute | solution.py:32
  58.7 9.3 %collective-permute-start.20 = (bf16[144,384]{1,0:T(8,128)(2,1)S(1)}, bf16[144,384]{1,0:T(8,128)(2,1)S(1)}, u32[]{:S(2)}, u32[]{:S(2)}) collective-permute-start(bf16[144,384]{1,0:T(8,128)(2,1)S(1)} %pad_maximum_fusion.8), channel_id=1, source_target_pairs={{0,6},{1,7},{2,4},{3,5},{4,2},{5,3},{6,0},{7,1},{8,14},{9,15},{10,... | collective-permute-start | bytes 331784 | tf_op jit(solution)/shard_map/ppermute | solution.py:32
  63.7 16.4 %collective-permute-start.23 = (bf16[64,1152]{1,0:T(8,128)(2,1)S(1)}, bf16[64,1152]{1,0:T(8,128)(2,1)S(1)}, u32[]{:S(2)}, u32[]{:S(2)}) collective-permute-start(bf16[64,1152]{1,0:T(8,128)(2,1)S(1)} %collective-permute-done.13.refs_0_), channel_id=1, source_target_pairs={{0,16},{16,0},{1,17},{17,1},{2,18},{18,2},{3,19},{19,3},{4,20},{20... | collective-permute-start | bytes 442376 | tf_op jit(solution)/shard_map/ppermute | solution.py:36
  63.7 17.6 %collective-permute-start.24 = (bf16[240,1152]{1,0:T(8,128)(2,1)S(1)}, bf16[240,1152]{1,0:T(8,128)(2,1)S(1)}, u32[]{:S(2)}, u32[]{:S(2)}) collective-permute-start(bf16[240,1152]{1,0:T(8,128)(2,1)S(1)} %collective-permute-done.14.refs_1_), channel_id=1, source_target_pairs={{0,16},{16,0},{1,17},{17,1},{2,18},{18,2},{3,19},{19,3},{4,20},{20... | collective-permute-start | bytes 1658888 | tf_op jit(solution)/shard_map/ppermute | solution.py:36
  68.0 11.7 %collective-permute-start.21 = (bf16[112,1152]{1,0:T(8,128)(2,1)S(1)}, bf16[112,1152]{1,0:T(8,128)(2,1)S(1)}, u32[]{:S(2)}, u32[]{:S(2)}) collective-permute-start(bf16[112,1152]{1,0:T(8,128)(2,1)S(1)} %slice_select_fusion.2), channel_id=1, source_target_pairs={{0,4},{1,5},{2,6},{3,7},{4,0},{5,1},{6,2},{7,3},{8,12},{9,13},{10,... | collective-permute-start | bytes 774152 | tf_op jit(solution)/shard_map/ppermute | solution.py:32
  68.6 12.7 %collective-permute-start.25 = (bf16[160,1152]{1,0:T(8,128)(2,1)S(1)}, bf16[160,1152]{1,0:T(8,128)(2,1)S(1)}, u32[]{:S(2)}, u32[]{:S(2)}) collective-permute-start(bf16[160,1152]{1,0:T(8,128)(2,1)S(1)} %collective-permute-done.17.refs_2_), channel_id=1, source_target_pairs={{0,16},{16,0},{1,17},{17,1},{2,18},{18,2},{3,19},{19,3},{4,20},{20... | collective-permute-start | bytes 1105928 | tf_op jit(solution)/shard_map/ppermute | solution.py:36
  70.5 8.4 %collective-permute-start.22 = (bf16[192,1152]{1,0:T(8,128)(2,1)S(1)}, bf16[192,1152]{1,0:T(8,128)(2,1)S(1)}, u32[]{:S(2)}, u32[]{:S(2)}) collective-permute-start(bf16[192,1152]{1,0:T(8,128)(2,1)S(1)} %get-tuple-element.65.refs_0_), channel_id=1, source_target_pairs={{0,1},{1,0},{2,3},{3,2},{4,5},{5,4},{6,7},{7,6},{8,9},{9,8},{10,11... | collective-permute-start | bytes 1327112 | tf_op jit(solution)/shard_map/ppermute | solution.py:32
  79.0 8.4 %collective-permute-start.27 = (bf16[192,1152]{1,0:T(8,128)(2,1)S(1)}, bf16[192,1152]{1,0:T(8,128)(2,1)S(1)}, u32[]{:S(2)}, u32[]{:S(2)}) collective-permute-start(bf16[192,1152]{1,0:T(8,128)(2,1)S(1)} %pad_maximum_fusion.2), channel_id=1, source_target_pairs={{0,2},{1,3},{2,0},{3,1},{4,6},{5,7},{6,4},{7,5},{8,10},{9,11},{10,... | collective-permute-start | bytes 1327112 | tf_op jit(solution)/shard_map/ppermute | solution.py:32
  80.0 12.0 %collective-permute-start.28 = (bf16[192,1152]{1,0:T(8,128)(2,1)S(1)}, bf16[192,1152]{1,0:T(8,128)(2,1)S(1)}, u32[]{:S(2)}, u32[]{:S(2)}) collective-permute-start(bf16[192,1152]{1,0:T(8,128)(2,1)S(1)} %pad_maximum_fusion.3), channel_id=1, source_target_pairs={{0,2},{1,3},{2,0},{3,1},{4,6},{5,7},{6,4},{7,5},{8,10},{9,11},{10,... | collective-permute-start | bytes 1327112 | tf_op jit(solution)/shard_map/ppermute | solution.py:32
  89.1 8.4 %collective-permute-start.29 = (bf16[192,1152]{1,0:T(8,128)(2,1)S(1)}, bf16[192,1152]{1,0:T(8,128)(2,1)S(1)}, u32[]{:S(2)}, u32[]{:S(2)}) collective-permute-start(bf16[192,1152]{1,0:T(8,128)(2,1)S(1)} %mlp_far0.1), channel_id=1, source_target_pairs={{0,2},{1,3},{2,0},{3,1},{4,6},{5,7},{6,4},{7,5},{8,10},{9,11},{10,... | collective-permute-start | bytes 1327112 | tf_op jit(solution)/shard_map/ppermute | solution.py:32
  93.8 11.1 %collective-permute-start.30 = (bf16[192,1152]{1,0:T(8,128)(2,1)S(1)}, bf16[192,1152]{1,0:T(8,128)(2,1)S(1)}, u32[]{:S(2)}, u32[]{:S(2)}) collective-permute-start(bf16[192,1152]{1,0:T(8,128)(2,1)S(1)} %mlp_far1.1), channel_id=1, source_target_pairs={{0,2},{1,3},{2,0},{3,1},{4,6},{5,7},{6,4},{7,5},{8,10},{9,11},{10,... | collective-permute-start | bytes 1327112 | tf_op jit(solution)/shard_map/ppermute | solution.py:32
  97.5 10.0 %collective-permute-start.31 = (bf16[96,1152]{1,0:T(8,128)(2,1)S(1)}, bf16[96,1152]{1,0:T(8,128)(2,1)S(1)}, u32[]{:S(2)}, u32[]{:S(2)}) collective-permute-start(bf16[96,1152]{1,0:T(8,128)(2,1)S(1)} %add_convert_fusion.1), channel_id=1, source_target_pairs={{0,1},{1,0},{2,3},{3,2},{4,5},{5,4},{6,7},{7,6},{8,9},{9,8},{10,11... | collective-permute-start | bytes 663560 | tf_op jit(solution)/shard_map/ppermute | solution.py:32
  105.0 6.5 %collective-permute-start.32 = (bf16[96,1152]{1,0:T(8,128)(2,1)S(1)}, bf16[96,1152]{1,0:T(8,128)(2,1)S(1)}, u32[]{:S(2)}, u32[]{:S(2)}) collective-permute-start(bf16[96,1152]{1,0:T(8,128)(2,1)S(1)} %add_convert_fusion), channel_id=1, source_target_pairs={{0,1},{1,0},{2,3},{3,2},{4,5},{5,4},{6,7},{7,6},{8,9},{9,8},{10,11... | collective-permute-start | bytes 663560 | tf_op jit(solution)/shard_map/ppermute | solution.py:32
  (21 other events, 133.4 us)
where the time goes:
time: 115 us
  waiting for transfers between devices  55.8 us (49%)
  starting transfers between devices  30.8 us (27%)
  Pallas kernels  22.9 us (20%)
  local copies, waits for them, and re-layouts  3.25 us (3%)
  other arithmetic  1.36 us (1%)
    ppermute x22, waiting for transfers between devices, permute_by(): return lax.ppermute(block, ('cfg', 'tok'), route)  53.9 us
    ppermute x22, starting transfers between devices, permute_by(): return lax.ppermute(block, ('cfg', 'tok'), route)  28.9 us
    pallas_call x9, Pallas kernels, call(): pl.pallas_call(kernel, out_shape=out_shape, in_specs=specs or [whole] * l...  22.9 us
  transfers between devices with their start and end apart: 34, of which 19 were waited for; matrix products, arithmetic and copies ran while one was open for 2% of the time, Pallas kernels for 18%

commit v1 on v0

--- a/solution.py
+++ b/solution.py
@@ -17,7 +17,8 @@
 SMALL = (4, 1, 2)
 PROJ = ((2, 4, 1), (4, 1, 2))
 HEADS_TO = ((2, 4, 1), (4, 1, 2))
-FAR_EARLY = (64, 240, 160)
+FAR_EARLY = (80, 64, 176, 128)
+CHUNKS = 3
 F32 = jnp.float32
 BF16 = jnp.bfloat16
 
@@ -258,7 +259,7 @@
     )
 
 
-def pack_kernel(up_ref, down_ref, *refs):
+def pack_kernel(row_counts, up_ref, down_ref, *refs):
     far_refs, (up_all, down_all, sems) = refs[:-3], refs[-3:]
     core, _, _ = place()
     hidden, parts = up_ref.shape[0], len(far_refs) // 2
@@ -273,10 +274,10 @@
         copies = []
         for d, dest in enumerate(dests):
             at = hidden
-            for ref in far_refs[parts * d : parts * (d + 1)]:
-                rows = ref.shape[0]
+            for rows, ref in zip(row_counts, far_refs[parts * d : parts * (d + 1)]):
+                source = ref.at[pl.ds(ref.shape[0] - rows, rows)]
                 copies.append(
-                    pltpu.make_async_copy(ref, dest.at[pl.ds(at, rows)], sems.at[len(copies)])
+                    pltpu.make_async_copy(source, dest.at[pl.ds(at, rows)], sems.at[len(copies)])
                 )
                 at += rows
         for copy in copies:
@@ -290,11 +291,11 @@
         copy.wait()
 
 
-def pack(up, down, far):
+def pack(up, down, far, row_counts):
     hidden, width = up.shape
     both = jax.ShapeDtypeStruct((2 * hidden, width), BF16)
     return call(
-        pack_kernel,
+        functools.partial(pack_kernel, row_counts),
         (both, both),
         (up, down) + tuple(far),
         scratch=[pltpu.SemaphoreType.DMA((2 + len(far),))],
@@ -336,15 +337,15 @@
 
 def final_kernel(
     counts_ref, guide_ref, coef_ref, mod_ref, mid_ref, part_ref, noisy_ref, weight_ref,
-    first_low, first_high, second_low, second_high, block_ref, pred_ref, base_ref, total,
+    *refs,
 ):
     core, latent, member = place()
     cap = mid_ref.shape[0]
-    half = cap // 2
-    for low, first, second in ((0, first_low, second_low), (half, first_high, second_high)):
-        total[low : low + half, :] = (
-            part_ref[low : low + half, :] + first[:half, :].astype(F32) + second[...].astype(F32)
-        )
+    sum_refs, (block_ref, pred_ref, base_ref, total) = refs[:-4], refs[-4:]
+    chunk = cap // CHUNKS
+    for i, (first, second) in enumerate(zip(sum_refs[:CHUNKS], sum_refs[CHUNKS:])):
+        rows = slice(i * chunk, (i + 1) * chunk)
+        total[rows, :] = part_ref[rows, :] + first[:chunk, :].astype(F32) + second[...].astype(F32)
     rows = (mid_ref[...] + mod_row(mod_ref, latent, 5) * total[...]).astype(BF16).astype(F32)
     count = counts_ref[latent, member]
     rows = jnp.where(lax.broadcasted_iota(jnp.int32, (cap, 1), 0) < count, rows, 0.0)
@@ -370,7 +371,7 @@
         (jax.ShapeDtypeStruct((cap, width), BF16), flat, flat),
         tuple(scalars) + (modulation, mid, part, noisy, weight) + tuple(firsts) + tuple(seconds),
         scratch=[pltpu.VMEM((cap, width), F32)],
-        specs=[smem] * 3 + [vmem] * 9,
+        specs=[smem] * 3 + [vmem] * (5 + 2 * CHUNKS),
         flops=2 * cap * width * weight.shape[0],
         name="finish",
     )
@@ -402,17 +403,19 @@
     large_rows, small_rows = own_rows[:large], own_rows[large:]
     hidden = up_t.shape[0]
     cuts = [sum(FAR_EARLY[:i]) for i in range(len(FAR_EARLY) + 1)] + [hidden]
+    sent = [jnp.where(core == 0, up_t[: cuts[1]], down_t[: cuts[1]])]
     proj_rows = None
     got, away = [], []
     for step in range(3):
         payload = large_rows if step == 0 else jnp.concatenate([large_rows, proj_rows])
         got_large = permute_by(payload, [order[step] for order in LARGE])
-        got_small = permute_by(small_rows, [SMALL[step]] * 2)
+        small_payload = jnp.concatenate([small_rows, sent[0]]) if step == 0 else small_rows
+        got_small = permute_by(small_payload, [SMALL[step]] * 2)
         if step == 0:
             up_t, down_t, _ = lax.optimization_barrier((up_t, down_t, got_large))
             sent = [
                 jnp.where(core == 0, up_t[low:high], down_t[low:high])
-                for low, high in zip(cuts[:-1], cuts[1:])
+                for low, high in zip(cuts[1:-1], cuts[2:])
             ]
             proj_own = [
                 lax.dynamic_slice_in_dim(proj_t, head * HEAD_DIM, HEAD_DIM) for head in (core, 1 - core)
@@ -436,11 +439,11 @@
             proj_rows = jnp.concatenate([proj_rows, got_large[4 * large :]])
         if step < 2:
             large_rows = jnp.concatenate([large_rows, got_large[: large << step]])
-            small_rows = jnp.concatenate([small_rows, got_small])
+            small_rows = jnp.concatenate([small_rows, got_small[: small << step]])
         got.append((got_large, got_small))
         away.append((from_other_half(got_large), from_other_half(got_small)))
     proj_last = permute_by(proj_rows, [order[2] for order in PROJ])
-    far = [permute_by(sent[0], [GROUP // 2] * 2)]
+    far = [got[0][1], permute_by(sent[0], [GROUP // 2] * 2)]
     late = qkv_rows(
         modulation,
         qkv_rows_t,
@@ -448,38 +451,40 @@
         (4 * large, 4 * small) * 2,
         "qkv_late",
     )
-    far.append(permute_by(after(sent[1], far[0], late), [GROUP // 2] * 2))
-    far.append(permute_by(after(sent[2], far[0], late), [GROUP // 2] * 2))
+    far.append(permute_by(after(sent[1], far[1], late), [GROUP // 2] * 2))
+    far.append(permute_by(after(sent[2], far[1], late), [GROUP // 2] * 2))
     mine, sent_heads = attention(piece_rows, early, late, cap)
     mate = permute_by(sent_heads, [order[2] for order in HEADS_TO])
-    mate, far[1], proj_last = lax.optimization_barrier((mate, far[1], proj_last))
+    mate, far[2], proj_last = lax.optimization_barrier((mate, far[2], proj_last))
     proj_parts = [proj_own[0], got[1][0], got[2][0], proj_last]
     proj_parts += [proj_own[1], away[1][0], away[2][0], from_other_half(proj_last)]
     plane = []
     for j in range(1, GROUP // 2):
         both = jnp.concatenate([a[:, j * cap : (j + 1) * cap] for a in (mine, mate)], axis=1)
         plane.append(permute_by(both, [spread(order, j) for order in HEADS_TO]))
-    far[2], *plane = lax.optimization_barrier((far[2], *plane))
+    far[3], *plane = lax.optimization_barrier((far[3], *plane))
     far.append(permute_by(after(sent[3], *plane), [GROUP // 2] * 2))
     mid, mlp_in = project(modulation, hidden_in, proj_parts, mine, mate, plane)
 
     side = permute_by(mlp_in, (1, 2))
+    chunk = cap // CHUNKS
     both = [
-        jnp.concatenate([rows[low : low + half] for rows in (mlp_in, side)]) for low in (0, half)
+        jnp.concatenate([rows[low : low + chunk] for rows in (mlp_in, side)])
+        for low in range(0, cap, chunk)
     ]
     across = [permute_by(rows, (2, 1)) for rows in both]
-    far[3] = after(far[3], *both)
-    far += [from_other_half(rows) for rows in far]
-    packed = pack(up_t, down_t, far)
+    far[4] = after(far[4], *both)
+    far += [away[0][1]] + [from_other_half(rows) for rows in far[1:]]
+    packed = pack(up_t, down_t, far, [high - low for low, high in zip(cuts[:-1], cuts[1:])])
     sums = [
-        mlp_rows((rows,), packed, (cap,), BF16, f"mlp_far{i}")[0] for i, rows in enumerate(across)
+        mlp_rows((rows,), packed, (2 * chunk,), BF16, f"mlp_far{i}")[0] for i, rows in enumerate(across)
     ]
     firsts = [permute_by(rows, (2, 1)) for rows in sums]
     part, *side_parts = mlp_rows(
-        (after(mlp_in, *sums), side), packed, (cap, half, half), F32, "mlp_near"
+        (after(mlp_in, *sums), side), packed, (cap,) + (chunk,) * CHUNKS, F32, "mlp_near"
     )
     seconds = [
-        permute_by((rows + first[half:].astype(F32)).astype(BF16), (1, 2))
+        permute_by((rows + first[chunk:].astype(F32)).astype(BF16), (1, 2))
         for rows, first in zip(side_parts, firsts)
     ]
     block_rows, pred, base = final(

time: 115 us -> 110 us (0.957)
  waiting for transfers between devices: 55.8 us -> 45.2 us
  starting transfers between devices: 30.8 us -> 33.1 us
  other arithmetic: 1.36 us -> 3.19 us
    ppermute x22 -> x25, waiting for transfers between devices: 53.9 us -> 43.5 us  [permute_by(): return lax.ppermute(block, ('cfg', 'tok'), route)]
    ppermute x22 -> x25, starting transfers between devices: 28.9 us -> 31.2 us  [permute_by(): return lax.ppermute(block, ('cfg', 'tok'), route)]
    pallas_call x9 -> x10, Pallas kernels: 22.9 us -> 23.8 us  [call(): pl.pallas_call(kernel, out_shape=out_shape, in_specs=specs or [whole] * l...]
  transfers between devices with their start and end apart: 34 -> 37, of which waited for: 19 -> 20; matrix products, arithmetic and copies ran while one was open for 2% -> 3% of each run, Pallas kernels for 18% -> 20%
where the time goes in v1:
time: 110 us
  waiting for transfers between devices  45.2 us (41%)
  starting transfers between devices  33.1 us (30%)
  Pallas kernels  23.8 us (22%)
  other arithmetic  3.19 us (3%)
  local copies, waits for them, and re-layouts  3.15 us (3%)
    ppermute x25, waiting for transfers between devices, permute_by(): return lax.ppermute(block, ('cfg', 'tok'), route)  43.5 us
    ppermute x25, starting transfers between devices, permute_by(): return lax.ppermute(block, ('cfg', 'tok'), route)  31.2 us
    pallas_call x10, Pallas kernels, call(): pl.pallas_call(kernel, out_shape=out_shape, in_specs=specs or [whole] * l...  23.8 us
  transfers between devices with their start and end apart: 37, of which 20 were waited for; matrix products, arithmetic and copies ran while one was open for 3% of the time, Pallas kernels for 20%

profile of v1, /device:TPU:0, one launch (start us, length us, event | category | flops | bytes accessed | tf_op | source)
XLA Modules:
  0.0 109.6 jit_solution(16784066546777275311)
XLA Ops:
  3.5 3.0 %collective-permute-start.2 = (bf16[112,1152]{1,0:T(8,128)(2,1)}, bf16[112,1152]{1,0:T(8,128)(2,1)S(1)}, u32[]{:S(2)}, u32[]{:S(2)}) collective-permute-start(bf16[112,1152]{1,0:T(8,128)(2,1)} %pad_maximum_fusion.6), channel_id=1, source_target_pairs={{0,4},{1,5},{2,6},{3,7},{4,0},{5,1},{6,2},{7,3},{8,12},{9,13},{10,... | collective-permute-start | bytes 774152 | tf_op jit(solution)/shard_map/ppermute | solution.py:33
  9.7 2.6 %collective-permute-done.refs_1_ = bf16[64,1152]{1,0:T(8,128)(2,1)S(1)} collective-permute-done((bf16[64,1152]{1,0:T(8,128)(2,1)S(1)}, bf16[64,1152]{1,0:T(8,128)(2,1)S(1)}, u32[]{:S(2)}, u32[]{:S(2)}) %collective-permute-start) | collective-permute-done | bytes 147488 | tf_op jit(solution)/shard_map/ppermute | solution.py:33
  15.7 3.6 %collective-permute-done.3.refs_4_ = bf16[64,1152]{1,0:T(8,128)(2,1)S(1)} collective-permute-done((bf16[64,1152]{1,0:T(8,128)(2,1)S(1)}, bf16[64,1152]{1,0:T(8,128)(2,1)S(1)}, u32[]{:S(2)}, u32[]{:S(2)}) %collective-permute-start.3) | collective-permute-done | bytes 147488 | tf_op jit(solution)/shard_map/ppermute | solution.py:33
  19.3 1.7 %collective-permute-done.1.refs_2_.refs_1_ = bf16[200,1152]{1,0:T(8,128)(2,1)S(1)} collective-permute-done((bf16[200,1152]{1,0:T(8,128)(2,1)S(1)}, bf16[200,1152]{1,0:T(8,128)(2,1)S(1)}, u32[]{:S(2)}, u32[]{:S(2)}) %collective-permute-start.1) | collective-permute-done | bytes 460832 | tf_op jit(solution)/shard_map/ppermute | solution.py:33
  22.7 1.9 %collective-permute-start.5 = (bf16[128,1152]{1,0:T(8,128)(2,1)S(1)}, bf16[128,1152]{1,0:T(8,128)(2,1)S(1)}, u32[]{:S(2)}, u32[]{:S(2)}) collective-permute-start(bf16[128,1152]{1,0:T(8,128)(2,1)S(1)} %pad_maximum_fusion.2), channel_id=1, source_target_pairs={{0,2},{1,3},{2,0},{3,1},{4,6},{5,7},{6,4},{7,5},{8,10},{9,11},{10,... | collective-permute-start | bytes 884744 | tf_op jit(solution)/shard_map/ppermute | solution.py:33
  24.7 2.5 %qkv_early.1.early_ref = bf16[768,768]{1,0:T(8,128)(2,1)S(1)} custom-call(f32[2,8,1152]{2,1,0:T(8,128)S(1)} %bitcast.33, bf16[432,1152]{1,0:T(8,128)(2,1)S(1)} %bitcast.39, bf16[192,1152]{1,0:T(8,128)(2,1)S(1)} %copy-done.2, bf16[64,1152]{1,0:T(8,128)(2,1)S(1)} %collective-permute-done.refs_1_, bf16[200,1152]{1,0:T(8,128)(2,1)S(1)} %collective-permute-done.1.refs_2_.refs_1_, ...), custom_call_target="tpu_custom_call" | custom-call | flops 1358954496 | bytes 3538944 | tf_op jit(solution)/shard_map/qkv_early/pallas_call | solution.py:62
  27.2 4.8 %collective-permute-done.5.refs_1_ = bf16[128,1152]{1,0:T(8,128)(2,1)S(1)} collective-permute-done((bf16[128,1152]{1,0:T(8,128)(2,1)S(1)}, bf16[128,1152]{1,0:T(8,128)(2,1)S(1)}, u32[]{:S(2)}, u32[]{:S(2)}) %collective-permute-start.5) | collective-permute-done | bytes 294944 | tf_op jit(solution)/shard_map/ppermute | solution.py:33
  31.9 2.6 %collective-permute-done.4.refs_0_.refs_2_ = bf16[400,1152]{1,0:T(8,128)(2,1)S(1)} collective-permute-done((bf16[400,1152]{1,0:T(8,128)(2,1)S(1)}, bf16[400,1152]{1,0:T(8,128)(2,1)S(1)}, u32[]{:S(2)}, u32[]{:S(2)}) %collective-permute-start.4) | collective-permute-done | bytes 921632 | tf_op jit(solution)/shard_map/ppermute | solution.py:33
  37.5 2.4 %qkv_late.1.late_ref = bf16[768,768]{1,0:T(8,128)(2,1)S(1)} custom-call(f32[2,8,1152]{2,1,0:T(8,128)S(1)} %bitcast.34, bf16[432,1152]{1,0:T(8,128)(2,1)S(1)} %bitcast.40, bf16[400,1152]{1,0:T(8,128)(2,1)S(1)} %collective-permute-done.4.refs_0_.refs_2_, bf16[128,1152]{1,0:T(8,128)(2,1)S(1)} %collective-permute-done.5.refs_1_, ...), custom_call_target="tpu_custom_call" | custom-call | flops 1358954496 | bytes 3502080 | tf_op jit(solution)/shard_map/qkv_late/pallas_call | solution.py:62
  39.9 2.4 %collective-permute-done.13.refs_1_ = bf16[64,1152]{1,0:T(8,128)(2,1)S(1)} collective-permute-done((bf16[64,1152]{1,0:T(8,128)(2,1)S(1)}, bf16[64,1152]{1,0:T(8,128)(2,1)S(1)}, u32[]{:S(2)}, u32[]{:S(2)}) %collective-permute-start.13) | collective-permute-done | bytes 147488 | tf_op jit(solution)/shard_map/ppermute | solution.py:33
  42.8 6.0 %attend.1 = (bf16[144,768]{1,0:T(8,128)(2,1)S(1)}, bf16[144,768]{1,0:T(8,128)(2,1)S(1)}) custom-call(s32[2,8]{1,0:T(2,128)S(1)} %copy-done.6, bf16[768,768]{1,0:T(8,128)(2,1)S(1)} %qkv_early.1.early_ref, bf16[768,768]{1,0:T(8,128)(2,1)S(1)} %qkv_late.1.late_ref), custom_call_target="tpu_custom_call" | custom-call | flops 1358954496 | bytes 2359360 | tf_op jit(solution)/shard_map/attend/pallas_call | solution.py:62
  50.0 2.0 %collective-permute-start.17 = (bf16[128,1152]{1,0:T(8,128)(2,1)S(1)}, bf16[128,1152]{1,0:T(8,128)(2,1)S(1)}, u32[]{:S(2)}, u32[]{:S(2)}) collective-permute-start(bf16[128,1152]{1,0:T(8,128)(2,1)S(1)} %get-tuple-element.53), channel_id=1, source_target_pairs={{0,4},{1,5},{2,6},{3,7},{4,0},{5,1},{6,2},{7,3},{8,12},{9,13},{10,... | collective-permute-start | bytes 884744 | tf_op jit(solution)/shard_map/ppermute | solution.py:33
  52.1 2.7 %collective-permute-done.12.mate_ref = bf16[144,768]{1,0:T(8,128)(2,1)S(1)} collective-permute-done((bf16[144,768]{1,0:T(8,128)(2,1)S(1)}, bf16[144,768]{1,0:T(8,128)(2,1)S(1)}, u32[]{:S(2)}, u32[]{:S(2)}) %collective-permute-start.12) | collective-permute-done | bytes 221216 | tf_op jit(solution)/shard_map/ppermute | solution.py:33
  56.4 1.6 %collective-permute-start.19 = (bf16[144,384]{1,0:T(8,128)(2,1)S(1)}, bf16[144,384]{1,0:T(8,128)(2,1)S(1)}, u32[]{:S(2)}, u32[]{:S(2)}) collective-permute-start(bf16[144,384]{1,0:T(8,128)(2,1)S(1)} %pad_maximum_fusion.9), channel_id=1, source_target_pairs={{0,4},{1,5},{2,6},{3,7},{4,0},{5,1},{6,2},{7,3},{8,12},{9,13},{10,... | collective-permute-start | bytes 331784 | tf_op jit(solution)/shard_map/ppermute | solution.py:33
  61.4 2.6 %collective-permute-done.20.refs_10_ = bf16[144,384]{1,0:T(8,128)(2,1)S(1)} collective-permute-done((bf16[144,384]{1,0:T(8,128)(2,1)S(1)}, bf16[144,384]{1,0:T(8,128)(2,1)S(1)}, u32[]{:S(2)}, u32[]{:S(2)}) %collective-permute-start.20) | collective-permute-done | bytes 110624 | tf_op jit(solution)/shard_map/ppermute | solution.py:33
  65.4 1.9 %project.1 = (f32[192,1152]{1,0:T(8,128)S(1)}, bf16[192,1152]{1,0:T(8,128)(2,1)S(1)}) custom-call(f32[2,8,1152]{2,1,0:T(8,128)S(1)} %bitcast.35, bf16[192,1152]{1,0:T(8,128)(2,1)S(1)} %copy-done.2, bf16[144,768]{1,0:T(8,128)(2,1)S(1)} %get-tuple-element.45.mine_ref, bf16[144,768]{1,0:T(8,128)(2,1)S(1)} %collective-permute-done.12.mate_ref, ...), custom_call_target="tpu_custom_call" | custom-call | flops 509607936 | bytes 5713920 | tf_op jit(solution)/shard_map/project/pallas_call | solution.py:62
  68.5 7.2 %collective-permute-done.22.refs_1_ = bf16[192,1152]{1,0:T(8,128)(2,1)S(1)} collective-permute-done((bf16[192,1152]{1,0:T(8,128)(2,1)S(1)}, bf16[192,1152]{1,0:T(8,128)(2,1)S(1)}, u32[]{:S(2)}, u32[]{:S(2)}) %collective-permute-start.22) | collective-permute-done | bytes 442400 | tf_op jit(solution)/shard_map/ppermute | solution.py:33
  79.1 1.9 %pack.1 = (bf16[1152,1152]{1,0:T(8,128)(2,1)S(1)}, bf16[1152,1152]{1,0:T(8,128)(2,1)S(1)}) custom-call(bf16[576,1152]{1,0:T(8,128)(2,1)S(1)} %bitcast.32, bf16[576,1152]{1,0:T(8,128)(2,1)S(1)} %bitcast.27, bf16[112,1152]{1,0:T(8,128)(2,1)S(1)} %collective-permute-done.2.refs_3_.refs_0_, bf16[64,1152]{1,0:T(8,128)(2,1)S(1)} %collective-permute-done.13.refs_1_, ...), custom_call_target="tpu_custom_call" | custom-call | bytes 5455872 | tf_op jit(solution)/shard_map/pack/pallas_call | solution.py:62
  81.0 1.8 %collective-permute-done.27.refs_0_ = bf16[128,1152]{1,0:T(8,128)(2,1)S(1)} collective-permute-done((bf16[128,1152]{1,0:T(8,128)(2,1)S(1)}, bf16[128,1152]{1,0:T(8,128)(2,1)S(1)}, u32[]{:S(2)}, u32[]{:S(2)}) %collective-permute-start.27) | collective-permute-done | bytes 294944 | tf_op jit(solution)/shard_map/ppermute | solution.py:33
  91.7 2.8 %mlp_near.1 = (f32[192,1152]{1,0:T(8,128)S(1)}, f32[64,1152]{1,0:T(8,128)S(1)}, f32[64,1152]{1,0:T(8,128)S(1)}, f32[64,1152]{1,0:T(8,128)S(1)}) custom-call(bf16[1152,1152]{1,0:T(8,128)(2,1)S(1)} %get-tuple-element.64.up_ref, bf16[1152,1152]{1,0:T(8,128)(2,1)S(1)} %get-tuple-element.65.down_ref, bf16[192,1152]{1,0:T(8,128)(2,1)S(1)} %get-tuple-element.66.refs_0_, ...), custom_call_target="tpu_custom_call" | custom-call | flops 2038431744 | bytes 6193152 | tf_op jit(solution)/shard_map/mlp_near/pallas_call | solution.py:62
  94.5 1.6 %collective-permute-start.33 = (bf16[64,1152]{1,0:T(8,128)(2,1)S(1)}, bf16[64,1152]{1,0:T(8,128)(2,1)S(1)}, u32[]{:S(2)}, u32[]{:S(2)}) collective-permute-start(bf16[64,1152]{1,0:T(8,128)(2,1)S(1)} %add_convert_fusion.2), channel_id=1, source_target_pairs={{0,1},{1,0},{2,3},{3,2},{4,5},{5,4},{6,7},{7,6},{8,9},{9,8},{10,11... | collective-permute-start | bytes 442376 | tf_op jit(solution)/shard_map/ppermute | solution.py:33
  96.7 3.9 %collective-permute-done.32.refs_2_ = bf16[128,1152]{1,0:T(8,128)(2,1)S(1)} collective-permute-done((bf16[128,1152]{1,0:T(8,128)(2,1)S(1)}, bf16[128,1152]{1,0:T(8,128)(2,1)S(1)}, u32[]{:S(2)}, u32[]{:S(2)}) %collective-permute-start.32) | collective-permute-done | bytes 294944 | tf_op jit(solution)/shard_map/ppermute | solution.py:33
  101.7 4.1 %collective-permute-done.35.refs_5_ = bf16[64,1152]{1,0:T(8,128)(2,1)S(1)} collective-permute-done((bf16[64,1152]{1,0:T(8,128)(2,1)S(1)}, bf16[64,1152]{1,0:T(8,128)(2,1)S(1)}, u32[]{:S(2)}, u32[]{:S(2)}) %collective-permute-start.35) | collective-permute-done | bytes 147488 | tf_op jit(solution)/shard_map/ppermute | solution.py:33
  105.8 1.9 %finish.1 = (bf16[192,1152]{1,0:T(8,128)(2,1)}, f32[16,192]{1,0:T(8,128)S(1)}, f32[16,192]{1,0:T(8,128)S(1)}) custom-call(s32[2,8]{1,0:T(2,128)S(1)} %copy-done.6, f32[2]{0:T(128)S(1)} %copy-done.8, f32[2,2]{1,0:T(2,128)S(1)} %copy-done.7, f32[2,8,1152]{2,1,0:T(8,128)S(1)} %bitcast.36, f32[192,1152]{1,0:T(8,128)S(1)} %get-tuple-element.57.mid_ref, ...), custom_call_target="tpu_custom_call" | custom-call | flops 7077888 | bytes 3219544 | tf_op jit(solution)/shard_map/finish/pallas_call | solution.py:62
  (115 shorter events, 38.9 us)
Async XLA Ops:
  3.5 10.5 %collective-permute-start.2 = (bf16[112,1152]{1,0:T(8,128)(2,1)}, bf16[112,1152]{1,0:T(8,128)(2,1)S(1)}, u32[]{:S(2)}, u32[]{:S(2)}) collective-permute-start(bf16[112,1152]{1,0:T(8,128)(2,1)} %pad_maximum_fusion.6), channel_id=1, source_target_pairs={{0,4},{1,5},{2,6},{3,7},{4,0},{5,1},{6,2},{7,3},{8,12},{9,13},{10,... | collective-permute-start | bytes 774152 | tf_op jit(solution)/shard_map/ppermute | solution.py:33
  12.4 8.6 %collective-permute-start.1 = (bf16[200,1152]{1,0:T(8,128)(2,1)S(1)}, bf16[200,1152]{1,0:T(8,128)(2,1)S(1)}, u32[]{:S(2)}, u32[]{:S(2)}) collective-permute-start(bf16[200,1152]{1,0:T(8,128)(2,1)S(1)} %pad_maximum_fusion.1), channel_id=1, source_target_pairs={{0,2},{1,3},{2,0},{3,1},{4,6},{5,7},{6,4},{7,5},{8,10},{9,11},{10,... | collective-permute-start | bytes 1382408 | tf_op jit(solution)/shard_map/ppermute | solution.py:33
  21.1 13.5 %collective-permute-start.4 = (bf16[400,1152]{1,0:T(8,128)(2,1)S(1)}, bf16[400,1152]{1,0:T(8,128)(2,1)S(1)}, u32[]{:S(2)}, u32[]{:S(2)}) collective-permute-start(bf16[400,1152]{1,0:T(8,128)(2,1)S(1)} %get-tuple-element.77), channel_id=1, source_target_pairs={{0,4},{1,5},{2,6},{3,7},{4,0},{5,1},{6,2},{7,3},{8,12},{9,13},{10,... | collective-permute-start | bytes 2764808 | tf_op jit(solution)/shard_map/ppermute | solution.py:33
  22.7 9.3 %collective-permute-start.5 = (bf16[128,1152]{1,0:T(8,128)(2,1)S(1)}, bf16[128,1152]{1,0:T(8,128)(2,1)S(1)}, u32[]{:S(2)}, u32[]{:S(2)}) collective-permute-start(bf16[128,1152]{1,0:T(8,128)(2,1)S(1)} %pad_maximum_fusion.2), channel_id=1, source_target_pairs={{0,2},{1,3},{2,0},{3,1},{4,6},{5,7},{6,4},{7,5},{8,10},{9,11},{10,... | collective-permute-start | bytes 884744 | tf_op jit(solution)/shard_map/ppermute | solution.py:33
  35.3 16.8 %collective-permute-start.15 = (bf16[288,1152]{1,0:T(8,128)(2,1)S(1)}, bf16[288,1152]{1,0:T(8,128)(2,1)S(1)}, u32[]{:S(2)}, u32[]{:S(2)}) collective-permute-start(bf16[288,1152]{1,0:T(8,128)(2,1)S(1)} %pad_maximum_fusion), channel_id=1, source_target_pairs={{0,1},{1,0},{2,3},{3,2},{4,5},{5,4},{6,7},{7,6},{8,9},{9,8},{10,11... | collective-permute-start | bytes 1990664 | tf_op jit(solution)/shard_map/ppermute | solution.py:33
  36.8 5.5 %collective-permute-start.13 = (bf16[64,1152]{1,0:T(8,128)(2,1)S(1)}, bf16[64,1152]{1,0:T(8,128)(2,1)S(1)}, u32[]{:S(2)}, u32[]{:S(2)}) collective-permute-start(bf16[64,1152]{1,0:T(8,128)(2,1)S(1)} %slice_select_fusion.4), channel_id=1, source_target_pairs={{0,4},{1,5},{2,6},{3,7},{4,0},{5,1},{6,2},{7,3},{8,12},{9,13},{10,... | collective-permute-start | bytes 442376 | tf_op jit(solution)/shard_map/ppermute | solution.py:33
  42.3 12.5 %collective-permute-start.14 = (bf16[176,1152]{1,0:T(8,128)(2,1)S(1)}, bf16[176,1152]{1,0:T(8,128)(2,1)S(1)}, u32[]{:S(2)}, u32[]{:S(2)}) collective-permute-start(bf16[176,1152]{1,0:T(8,128)(2,1)S(1)} %slice_select_fusion), channel_id=1, source_target_pairs={{0,4},{1,5},{2,6},{3,7},{4,0},{5,1},{6,2},{7,3},{8,12},{9,13},{10,... | collective-permute-start | bytes 1216520 | tf_op jit(solution)/shard_map/ppermute | solution.py:33
  48.8 6.0 %collective-permute-start.12 = (bf16[144,768]{1,0:T(8,128)(2,1)S(1)}, bf16[144,768]{1,0:T(8,128)(2,1)S(1)}, u32[]{:S(2)}, u32[]{:S(2)}) collective-permute-start(bf16[144,768]{1,0:T(8,128)(2,1)S(1)} %get-tuple-element.46), channel_id=1, source_target_pairs={{0,1},{1,0},{2,3},{3,2},{4,5},{5,4},{6,7},{7,6},{8,9},{9,8},{10,11... | collective-permute-start | bytes 663560 | tf_op jit(solution)/shard_map/ppermute | solution.py:33
  50.0 9.4 %collective-permute-start.17 = (bf16[128,1152]{1,0:T(8,128)(2,1)S(1)}, bf16[128,1152]{1,0:T(8,128)(2,1)S(1)}, u32[]{:S(2)}, u32[]{:S(2)}) collective-permute-start(bf16[128,1152]{1,0:T(8,128)(2,1)S(1)} %get-tuple-element.53), channel_id=1, source_target_pairs={{0,4},{1,5},{2,6},{3,7},{4,0},{5,1},{6,2},{7,3},{8,12},{9,13},{10,... | collective-permute-start | bytes 884744 | tf_op jit(solution)/shard_map/ppermute | solution.py:33
  54.8 10.6 %collective-permute-start.16 = (bf16[288,1152]{1,0:T(8,128)(2,1)S(1)}, bf16[288,1152]{1,0:T(8,128)(2,1)S(1)}, u32[]{:S(2)}, u32[]{:S(2)}) collective-permute-start(bf16[288,1152]{1,0:T(8,128)(2,1)S(1)} %collective-permute-done.15.refs_3_), channel_id=1, source_target_pairs={{0,16},{16,0},{1,17},{17,1},{2,18},{18,2},{3,19},{19,3},{4,20},{20... | collective-permute-start | bytes 1990664 | tf_op jit(solution)/shard_map/ppermute | solution.py:37
  58.1 5.9 %collective-permute-start.20 = (bf16[144,384]{1,0:T(8,128)(2,1)S(1)}, bf16[144,384]{1,0:T(8,128)(2,1)S(1)}, u32[]{:S(2)}, u32[]{:S(2)}) collective-permute-start(bf16[144,384]{1,0:T(8,128)(2,1)S(1)} %pad_maximum_fusion.10), channel_id=1, source_target_pairs={{0,6},{1,7},{2,4},{3,5},{4,2},{5,3},{6,0},{7,1},{8,14},{9,15},{10,... | collective-permute-start | bytes 331784 | tf_op jit(solution)/shard_map/ppermute | solution.py:33
  59.4 17.7 %collective-permute-start.23 = (bf16[64,1152]{1,0:T(8,128)(2,1)S(1)}, bf16[64,1152]{1,0:T(8,128)(2,1)S(1)}, u32[]{:S(2)}, u32[]{:S(2)}) collective-permute-start(bf16[64,1152]{1,0:T(8,128)(2,1)S(1)} %collective-permute-done.13.refs_1_), channel_id=1, source_target_pairs={{0,16},{16,0},{1,17},{17,1},{2,18},{18,2},{3,19},{19,3},{4,20},{20... | collective-permute-start | bytes 442376 | tf_op jit(solution)/shard_map/ppermute | solution.py:37
  59.9 19.3 %collective-permute-start.24 = (bf16[176,1152]{1,0:T(8,128)(2,1)S(1)}, bf16[176,1152]{1,0:T(8,128)(2,1)S(1)}, u32[]{:S(2)}, u32[]{:S(2)}) collective-permute-start(bf16[176,1152]{1,0:T(8,128)(2,1)S(1)} %collective-permute-done.14.refs_2_), channel_id=1, source_target_pairs={{0,16},{16,0},{1,17},{17,1},{2,18},{18,2},{3,19},{19,3},{4,20},{20... | collective-permute-start | bytes 1216520 | tf_op jit(solution)/shard_map/ppermute | solution.py:37
  64.0 11.9 %collective-permute-start.21 = (bf16[128,1152]{1,0:T(8,128)(2,1)S(1)}, bf16[128,1152]{1,0:T(8,128)(2,1)S(1)}, u32[]{:S(2)}, u32[]{:S(2)}) collective-permute-start(bf16[128,1152]{1,0:T(8,128)(2,1)S(1)} %get-tuple-element.61), channel_id=1, source_target_pairs={{0,4},{1,5},{2,6},{3,7},{4,0},{5,1},{6,2},{7,3},{8,12},{9,13},{10,... | collective-permute-start | bytes 884744 | tf_op jit(solution)/shard_map/ppermute | solution.py:33
  65.4 12.6 %collective-permute-start.25 = (bf16[128,1152]{1,0:T(8,128)(2,1)S(1)}, bf16[128,1152]{1,0:T(8,128)(2,1)S(1)}, u32[]{:S(2)}, u32[]{:S(2)}) collective-permute-start(bf16[128,1152]{1,0:T(8,128)(2,1)S(1)} %collective-permute-done.17.refs_3_), channel_id=1, source_target_pairs={{0,16},{16,0},{1,17},{17,1},{2,18},{18,2},{3,19},{19,3},{4,20},{20... | collective-permute-start | bytes 884744 | tf_op jit(solution)/shard_map/ppermute | solution.py:37
  67.4 8.4 %collective-permute-start.22 = (bf16[192,1152]{1,0:T(8,128)(2,1)S(1)}, bf16[192,1152]{1,0:T(8,128)(2,1)S(1)}, u32[]{:S(2)}, u32[]{:S(2)}) collective-permute-start(bf16[192,1152]{1,0:T(8,128)(2,1)S(1)} %get-tuple-element.66.refs_0_), channel_id=1, source_target_pairs={{0,1},{1,0},{2,3},{3,2},{4,5},{5,4},{6,7},{7,6},{8,9},{9,8},{10,11... | collective-permute-start | bytes 1327112 | tf_op jit(solution)/shard_map/ppermute | solution.py:33
  76.0 6.8 %collective-permute-start.27 = (bf16[128,1152]{1,0:T(8,128)(2,1)S(1)}, bf16[128,1152]{1,0:T(8,128)(2,1)S(1)}, u32[]{:S(2)}, u32[]{:S(2)}) collective-permute-start(bf16[128,1152]{1,0:T(8,128)(2,1)S(1)} %pad_maximum_fusion.3), channel_id=1, source_target_pairs={{0,2},{1,3},{2,0},{3,1},{4,6},{5,7},{6,4},{7,5},{8,10},{9,11},{10,... | collective-permute-start | bytes 884744 | tf_op jit(solution)/shard_map/ppermute | solution.py:33
  77.1 8.8 %collective-permute-start.28 = (bf16[128,1152]{1,0:T(8,128)(2,1)S(1)}, bf16[128,1152]{1,0:T(8,128)(2,1)S(1)}, u32[]{:S(2)}, u32[]{:S(2)}) collective-permute-start(bf16[128,1152]{1,0:T(8,128)(2,1)S(1)} %pad_maximum_fusion.4), channel_id=1, source_target_pairs={{0,2},{1,3},{2,0},{3,1},{4,6},{5,7},{6,4},{7,5},{8,10},{9,11},{10,... | collective-permute-start | bytes 884744 | tf_op jit(solution)/shard_map/ppermute | solution.py:33
  78.1 11.0 %collective-permute-start.29 = (bf16[128,1152]{1,0:T(8,128)(2,1)S(1)}, bf16[128,1152]{1,0:T(8,128)(2,1)S(1)}, u32[]{:S(2)}, u32[]{:S(2)}) collective-permute-start(bf16[128,1152]{1,0:T(8,128)(2,1)S(1)} %pad_maximum_fusion.5), channel_id=1, source_target_pairs={{0,2},{1,3},{2,0},{3,1},{4,6},{5,7},{6,4},{7,5},{8,10},{9,11},{10,... | collective-permute-start | bytes 884744 | tf_op jit(solution)/shard_map/ppermute | solution.py:33
  84.2 10.2 %collective-permute-start.30 = (bf16[128,1152]{1,0:T(8,128)(2,1)S(1)}, bf16[128,1152]{1,0:T(8,128)(2,1)S(1)}, u32[]{:S(2)}, u32[]{:S(2)}) collective-permute-start(bf16[128,1152]{1,0:T(8,128)(2,1)S(1)} %mlp_far0.1), channel_id=1, source_target_pairs={{0,2},{1,3},{2,0},{3,1},{4,6},{5,7},{6,4},{7,5},{8,10},{9,11},{10,... | collective-permute-start | bytes 884744 | tf_op jit(solution)/shard_map/ppermute | solution.py:33
  87.4 8.8 %collective-permute-start.31 = (bf16[128,1152]{1,0:T(8,128)(2,1)S(1)}, bf16[128,1152]{1,0:T(8,128)(2,1)S(1)}, u32[]{:S(2)}, u32[]{:S(2)}) collective-permute-start(bf16[128,1152]{1,0:T(8,128)(2,1)S(1)} %mlp_far1.1), channel_id=1, source_target_pairs={{0,2},{1,3},{2,0},{3,1},{4,6},{5,7},{6,4},{7,5},{8,10},{9,11},{10,... | collective-permute-start | bytes 884744 | tf_op jit(solution)/shard_map/ppermute | solution.py:33
  90.6 10.0 %collective-permute-start.32 = (bf16[128,1152]{1,0:T(8,128)(2,1)S(1)}, bf16[128,1152]{1,0:T(8,128)(2,1)S(1)}, u32[]{:S(2)}, u32[]{:S(2)}) collective-permute-start(bf16[128,1152]{1,0:T(8,128)(2,1)S(1)} %mlp_far2.1), channel_id=1, source_target_pairs={{0,2},{1,3},{2,0},{3,1},{4,6},{5,7},{6,4},{7,5},{8,10},{9,11},{10,... | collective-permute-start | bytes 884744 | tf_op jit(solution)/shard_map/ppermute | solution.py:33
  94.5 7.2 %collective-permute-start.33 = (bf16[64,1152]{1,0:T(8,128)(2,1)S(1)}, bf16[64,1152]{1,0:T(8,128)(2,1)S(1)}, u32[]{:S(2)}, u32[]{:S(2)}) collective-permute-start(bf16[64,1152]{1,0:T(8,128)(2,1)S(1)} %add_convert_fusion.2), channel_id=1, source_target_pairs={{0,1},{1,0},{2,3},{3,2},{4,5},{5,4},{6,7},{7,6},{8,9},{9,8},{10,11... | collective-permute-start | bytes 442376 | tf_op jit(solution)/shard_map/ppermute | solution.py:33
  96.2 5.6 %collective-permute-start.34 = (bf16[64,1152]{1,0:T(8,128)(2,1)S(1)}, bf16[64,1152]{1,0:T(8,128)(2,1)S(1)}, u32[]{:S(2)}, u32[]{:S(2)}) collective-permute-start(bf16[64,1152]{1,0:T(8,128)(2,1)S(1)} %add_convert_fusion.1), channel_id=1, source_target_pairs={{0,1},{1,0},{2,3},{3,2},{4,5},{5,4},{6,7},{7,6},{8,9},{9,8},{10,11... | collective-permute-start | bytes 442376 | tf_op jit(solution)/shard_map/ppermute | solution.py:33
  (24 other events, 139.4 us)

commit v2 on v1

--- a/solution.py
+++ b/solution.py
@@ -17,7 +17,7 @@
 SMALL = (4, 1, 2)
 PROJ = ((2, 4, 1), (4, 1, 2))
 HEADS_TO = ((2, 4, 1), (4, 1, 2))
-FAR_EARLY = (80, 64, 176, 128)
+FAR_EARLY = 416
 CHUNKS = 3
 F32 = jnp.float32
 BF16 = jnp.bfloat16
@@ -120,7 +120,8 @@
     return sum(bit for i, bit in enumerate(order) if index >> i & 1)
 
 
-def attention_kernel(cap, packed_rows, counts_ref, early_ref, late_ref, near_ref, far_ref, packed, out):
+def attention_kernel(cap, packed_rows, counts_ref, early_ref, *refs):
+    late_refs, (near_ref, far_ref, packed, out) = refs[:2], refs[2:]
     core, latent, member = place()
     half = cap // 2
     large, small = 2 * half // 3, half // 3
@@ -133,24 +134,28 @@
     total_rows = packed.shape[0]
     spare = total_rows - LEN
     packed[LEN:, :] = jnp.zeros((spare, packed.shape[1]), BF16)
-    for d in range(GROUP):
-        for k in range(2):
-            away = (core != k).astype(jnp.int32)
-            for is_small in range(2):
-                size = small if is_small else large
-                first = k * half + is_small * large
-                where = position(SMALL if is_small else LARGE[k], d)
-                if where == 0:
-                    rows = early_ref[first : first + size, :]
-                elif where < 4:
-                    base = cap + is_small * 3 * large + (where - 1) * size
-                    base = pl.multiple_of(base + away * (3 * half), 32)
-                    rows = early_ref[pl.ds(base, size), :]
-                else:
-                    base = is_small * 4 * large + (where - 4) * size
-                    base = pl.multiple_of(base + away * (4 * half), 32)
-                    rows = late_ref[pl.ds(base, size), :]
-                packed[pl.ds(pl.multiple_of(starts[d] + first, ALIGN), size), :] = rows
+    def lay(own_core):
+        for d in range(GROUP):
+            for k in range(2):
+                away = own_core != k
+                for is_small in range(2):
+                    size = small if is_small else large
+                    first = k * half + is_small * large
+                    where = position(SMALL if is_small else LARGE[k], d)
+                    source = early_ref
+                    if where == 0:
+                        base = first
+                    elif where < 4:
+                        base = cap + is_small * 3 * large + (where - 1) * size + away * 3 * half
+                    else:
+                        source = late_refs[away]
+                        base = is_small * 4 * large + (where - 4) * size
+                    packed[pl.ds(pl.multiple_of(starts[d] + first, ALIGN), size), :] = source[
+                        base : base + size, :
+                    ]
+
+    pl.when(core == 0)(lambda: lay(0))
+    pl.when(core == 1)(lambda: lay(1))
     slot = lax.broadcasted_iota(jnp.int32, (1, packed_rows), 1)
     valid = jnp.zeros((1, packed_rows), jnp.bool_)
     for d in range(GROUP):
@@ -199,9 +204,9 @@
     return call(
         functools.partial(attention_kernel, cap, packed_rows),
         (shape, shape),
-        (piece_rows, early, late),
+        (piece_rows, early) + tuple(late),
         scratch=[pltpu.VMEM((total, 3 * width), BF16), pltpu.VMEM((total, width), F32)],
-        specs=[pl.BlockSpec(memory_space=pltpu.SMEM)] + [pl.BlockSpec(memory_space=pltpu.VMEM)] * 2,
+        specs=[pl.BlockSpec(memory_space=pltpu.SMEM)] + [pl.BlockSpec(memory_space=pltpu.VMEM)] * 3,
         flops=4 * heads * packed_rows * packed_rows * LANES,
         name="attend",
     )
@@ -402,20 +407,18 @@
     own_rows = after(lax.dynamic_slice_in_dim(hidden_in, core * half, half))
     large_rows, small_rows = own_rows[:large], own_rows[large:]
     hidden = up_t.shape[0]
-    cuts = [sum(FAR_EARLY[:i]) for i in range(len(FAR_EARLY) + 1)] + [hidden]
-    sent = [jnp.where(core == 0, up_t[: cuts[1]], down_t[: cuts[1]])]
+    cuts = (0, FAR_EARLY, hidden)
     proj_rows = None
     got, away = [], []
     for step in range(3):
         payload = large_rows if step == 0 else jnp.concatenate([large_rows, proj_rows])
         got_large = permute_by(payload, [order[step] for order in LARGE])
-        small_payload = jnp.concatenate([small_rows, sent[0]]) if step == 0 else small_rows
-        got_small = permute_by(small_payload, [SMALL[step]] * 2)
+        got_small = permute_by(small_rows, [SMALL[step]] * 2)
         if step == 0:
             up_t, down_t, _ = lax.optimization_barrier((up_t, down_t, got_large))
             sent = [
                 jnp.where(core == 0, up_t[low:high], down_t[low:high])
-                for low, high in zip(cuts[1:-1], cuts[2:])
+                for low, high in zip(cuts[:-1], cuts[1:])
             ]
             proj_own = [
                 lax.dynamic_slice_in_dim(proj_t, head * HEAD_DIM, HEAD_DIM) for head in (core, 1 - core)
@@ -439,42 +442,36 @@
             proj_rows = jnp.concatenate([proj_rows, got_large[4 * large :]])
         if step < 2:
             large_rows = jnp.concatenate([large_rows, got_large[: large << step]])
-            small_rows = jnp.concatenate([small_rows, got_small[: small << step]])
+            small_rows = jnp.concatenate([small_rows, got_small])
         got.append((got_large, got_small))
         away.append((from_other_half(got_large), from_other_half(got_small)))
     proj_last = permute_by(proj_rows, [order[2] for order in PROJ])
-    far = [got[0][1], permute_by(sent[0], [GROUP // 2] * 2)]
-    late = qkv_rows(
-        modulation,
-        qkv_rows_t,
-        got[2] + away[2],
-        (4 * large, 4 * small) * 2,
-        "qkv_late",
-    )
-    far.append(permute_by(after(sent[1], far[1], late), [GROUP // 2] * 2))
-    far.append(permute_by(after(sent[2], far[1], late), [GROUP // 2] * 2))
+    far = [permute_by(sent[0], [GROUP // 2] * 2)]
+    late = [qkv_rows(modulation, qkv_rows_t, got[2], (4 * large, 4 * small), "qkv_late_own")]
+    *other, late[0] = lax.optimization_barrier((*away[2], late[0]))
+    late.append(qkv_rows(modulation, qkv_rows_t, other, (4 * large, 4 * small), "qkv_late_other"))
     mine, sent_heads = attention(piece_rows, early, late, cap)
     mate = permute_by(sent_heads, [order[2] for order in HEADS_TO])
-    mate, far[2], proj_last = lax.optimization_barrier((mate, far[2], proj_last))
+    mate, proj_last = lax.optimization_barrier((mate, proj_last))
     proj_parts = [proj_own[0], got[1][0], got[2][0], proj_last]
     proj_parts += [proj_own[1], away[1][0], away[2][0], from_other_half(proj_last)]
     plane = []
     for j in range(1, GROUP // 2):
         both = jnp.concatenate([a[:, j * cap : (j + 1) * cap] for a in (mine, mate)], axis=1)
         plane.append(permute_by(both, [spread(order, j) for order in HEADS_TO]))
-    far[3], *plane = lax.optimization_barrier((far[3], *plane))
-    far.append(permute_by(after(sent[3], *plane), [GROUP // 2] * 2))
+    far[0], *plane = lax.optimization_barrier((far[0], *plane))
+    far.append(permute_by(after(sent[1], *plane), [GROUP // 2] * 2))
     mid, mlp_in = project(modulation, hidden_in, proj_parts, mine, mate, plane)
 
+    chunk = cap // CHUNKS
     side = permute_by(mlp_in, (1, 2))
-    chunk = cap // CHUNKS
     both = [
         jnp.concatenate([rows[low : low + chunk] for rows in (mlp_in, side)])
         for low in range(0, cap, chunk)
     ]
     across = [permute_by(rows, (2, 1)) for rows in both]
-    far[4] = after(far[4], *both)
-    far += [away[0][1]] + [from_other_half(rows) for rows in far[1:]]
+    far[1] = after(far[1], *both)
+    far += [from_other_half(rows) for rows in far]
     packed = pack(up_t, down_t, far, [high - low for low, high in zip(cuts[:-1], cuts[1:])])
     sums = [
         mlp_rows((rows,), packed, (2 * chunk,), BF16, f"mlp_far{i}")[0] for i, rows in enumerate(across)

time: 110 us -> 107 us (0.973)
  starting transfers between devices: 33.1 us -> 29.7 us
  waiting for transfers between devices: 45.2 us -> 47.8 us
  other arithmetic: 3.19 us -> 1.35 us
    ppermute x25 -> x23, starting transfers between devices: 31.2 us -> 27.9 us  [permute_by(): return lax.ppermute(block, ('cfg', 'tok'), route)]
    ppermute x25 -> x23, waiting for transfers between devices: 43.5 us -> 46.6 us  [permute_by(): return lax.ppermute(block, ('cfg', 'tok'), route)]
    select_n x1 -> x0, other arithmetic: 1.14 us -> none  [shards(): sent = [jnp.where(core == 0, up_t[:cuts[1]], down_t[:cuts[1]])]]
    pallas_call x10 -> x11, Pallas kernels: 23.8 us -> 24.4 us  [call(): pl.pallas_call(kernel, out_shape=out_shape, in_specs=specs or [whole] * l...]
  transfers between devices with their start and end apart: 37 -> 33, of which waited for: 20 -> 16; matrix products, arithmetic and copies ran while one was open for 3% -> 2% of each run, Pallas kernels for 20% -> 21%
where the time goes in v2:
time: 107 us
  waiting for transfers between devices  47.8 us (45%)
  starting transfers between devices  29.7 us (28%)
  Pallas kernels  24.4 us (23%)
  local copies, waits for them, and re-layouts  2.48 us (2%)
  other arithmetic  1.35 us (1%)
  between operations  1.07 us (1%)
    ppermute x23, waiting for transfers between devices, permute_by(): return lax.ppermute(block, ('cfg', 'tok'), route)  46.6 us
    ppermute x23, starting transfers between devices, permute_by(): return lax.ppermute(block, ('cfg', 'tok'), route)  27.9 us
    pallas_call x11, Pallas kernels, call(): pl.pallas_call(kernel, out_shape=out_shape, in_specs=specs or [whole] * l...  24.4 us
  transfers between devices with their start and end apart: 33, of which 16 were waited for; matrix products, arithmetic and copies ran while one was open for 2% of the time, Pallas kernels for 21%

profile of v2, /device:TPU:0, one launch (start us, length us, event | category | flops | bytes accessed | tf_op | source)
XLA Modules:
  0.0 106.8 jit_solution(2117833744420867534)
XLA Ops:
  1.6 3.1 %collective-permute-start.2 = (bf16[32,1152]{1,0:T(8,128)(2,1)S(1)}, bf16[32,1152]{1,0:T(8,128)(2,1)S(1)}, u32[]{:S(2)}, u32[]{:S(2)}) collective-permute-start(bf16[32,1152]{1,0:T(8,128)(2,1)S(1)} %slice.97), channel_id=1, source_target_pairs={{0,4},{1,5},{2,6},{3,7},{4,0},{5,1},{6,2},{7,3},{8,12},{9,13},{10,... | collective-permute-start | bytes 221192 | tf_op jit(solution)/shard_map/ppermute | solution.py:33
  7.3 2.6 %collective-permute-done.refs_1_ = bf16[64,1152]{1,0:T(8,128)(2,1)S(1)} collective-permute-done((bf16[64,1152]{1,0:T(8,128)(2,1)S(1)}, bf16[64,1152]{1,0:T(8,128)(2,1)S(1)}, u32[]{:S(2)}, u32[]{:S(2)}) %collective-permute-start) | collective-permute-done | bytes 147488 | tf_op jit(solution)/shard_map/ppermute | solution.py:33
  10.0 1.6 %collective-permute-start.1 = (bf16[200,1152]{1,0:T(8,128)(2,1)S(1)}, bf16[200,1152]{1,0:T(8,128)(2,1)S(1)}, u32[]{:S(2)}, u32[]{:S(2)}) collective-permute-start(bf16[200,1152]{1,0:T(8,128)(2,1)S(1)} %pad_maximum_fusion.1), channel_id=1, source_target_pairs={{0,2},{1,3},{2,0},{3,1},{4,6},{5,7},{6,4},{7,5},{8,10},{9,11},{10,... | collective-permute-start | bytes 1382408 | tf_op jit(solution)/shard_map/ppermute | solution.py:33
  13.2 3.6 %collective-permute-done.3.refs_4_ = bf16[64,1152]{1,0:T(8,128)(2,1)S(1)} collective-permute-done((bf16[64,1152]{1,0:T(8,128)(2,1)S(1)}, bf16[64,1152]{1,0:T(8,128)(2,1)S(1)}, u32[]{:S(2)}, u32[]{:S(2)}) %collective-permute-start.3) | collective-permute-done | bytes 147488 | tf_op jit(solution)/shard_map/ppermute | solution.py:33
  16.8 1.8 %collective-permute-done.1.refs_2_.refs_1_ = bf16[200,1152]{1,0:T(8,128)(2,1)S(1)} collective-permute-done((bf16[200,1152]{1,0:T(8,128)(2,1)S(1)}, bf16[200,1152]{1,0:T(8,128)(2,1)S(1)}, u32[]{:S(2)}, u32[]{:S(2)}) %collective-permute-start.1) | collective-permute-done | bytes 460832 | tf_op jit(solution)/shard_map/ppermute | solution.py:33
  19.6 2.0 %collective-permute-start.5 = (bf16[128,1152]{1,0:T(8,128)(2,1)S(1)}, bf16[128,1152]{1,0:T(8,128)(2,1)S(1)}, u32[]{:S(2)}, u32[]{:S(2)}) collective-permute-start(bf16[128,1152]{1,0:T(8,128)(2,1)S(1)} %pad_maximum_fusion.2), channel_id=1, source_target_pairs={{0,2},{1,3},{2,0},{3,1},{4,6},{5,7},{6,4},{7,5},{8,10},{9,11},{10,... | collective-permute-start | bytes 884744 | tf_op jit(solution)/shard_map/ppermute | solution.py:33
  21.7 2.5 %qkv_early.1.early_ref = bf16[768,768]{1,0:T(8,128)(2,1)S(1)} custom-call(f32[2,8,1152]{2,1,0:T(8,128)S(1)} %bitcast.32, bf16[432,1152]{1,0:T(8,128)(2,1)S(1)} %bitcast.29, bf16[192,1152]{1,0:T(8,128)(2,1)S(1)} %copy-done.4, bf16[64,1152]{1,0:T(8,128)(2,1)S(1)} %collective-permute-done.refs_1_, bf16[200,1152]{1,0:T(8,128)(2,1)S(1)} %collective-permute-done.1.refs_2_.refs_1_, ...), custom_call_target="tpu_custom_call" | custom-call | flops 1358954496 | bytes 3170304 | tf_op jit(solution)/shard_map/qkv_early/pallas_call | solution.py:62
  24.2 5.0 %collective-permute-done.5.refs_1_ = bf16[128,1152]{1,0:T(8,128)(2,1)S(1)} collective-permute-done((bf16[128,1152]{1,0:T(8,128)(2,1)S(1)}, bf16[128,1152]{1,0:T(8,128)(2,1)S(1)}, u32[]{:S(2)}, u32[]{:S(2)}) %collective-permute-start.5) | collective-permute-done | bytes 294944 | tf_op jit(solution)/shard_map/ppermute | solution.py:33
  29.2 3.0 %collective-permute-done.4.refs_0_.refs_2_ = bf16[400,1152]{1,0:T(8,128)(2,1)S(1)} collective-permute-done((bf16[400,1152]{1,0:T(8,128)(2,1)S(1)}, bf16[400,1152]{1,0:T(8,128)(2,1)S(1)}, u32[]{:S(2)}, u32[]{:S(2)}) %collective-permute-start.4) | collective-permute-done | bytes 921632 | tf_op jit(solution)/shard_map/ppermute | solution.py:33
  34.8 1.7 %qkv_late_own.1.refs_0_ = bf16[384,768]{1,0:T(8,128)(2,1)S(1)} custom-call(f32[2,8,1152]{2,1,0:T(8,128)S(1)} %bitcast.33, bf16[432,1152]{1,0:T(8,128)(2,1)S(1)} %bitcast.30, bf16[400,1152]{1,0:T(8,128)(2,1)S(1)} %collective-permute-done.4.refs_0_.refs_2_, bf16[128,1152]{1,0:T(8,128)(2,1)S(1)} %collective-permute-done.5.refs_1_), custom_call_target="tpu_custom_call" | custom-call | flops 679477248 | bytes 2285568 | tf_op jit(solution)/shard_map/qkv_late_own/pallas_call | solution.py:62
  36.5 1.7 %qkv_late_other.1.refs_1_ = bf16[384,768]{1,0:T(8,128)(2,1)S(1)} custom-call(f32[2,8,1152]{2,1,0:T(8,128)S(1)} %bitcast.34, bf16[432,1152]{1,0:T(8,128)(2,1)S(1)} %bitcast.31, bf16[400,1152]{1,0:T(8,128)(2,1)S(1)} %collective-permute-done.10.refs_0_.refs_6_, bf16[128,1152]{1,0:T(8,128)(2,1)S(1)} %collective-permute-done.11.refs_1_), custom_call_target="tpu_custom_call" | custom-call | flops 679477248 | bytes 2285568 | tf_op jit(solution)/shard_map/qkv_late_other/pallas_call | solution.py:62
  38.2 6.2 %attend.1 = (bf16[144,768]{1,0:T(8,128)(2,1)S(1)}, bf16[144,768]{1,0:T(8,128)(2,1)S(1)}) custom-call(s32[2,8]{1,0:T(2,128)S(1)} %copy-done.7, bf16[768,768]{1,0:T(8,128)(2,1)S(1)} %qkv_early.1.early_ref, bf16[384,768]{1,0:T(8,128)(2,1)S(1)} %qkv_late_own.1.refs_0_, bf16[384,768]{1,0:T(8,128)(2,1)S(1)} %qkv_late_other.1.refs_1_), custom_call_target="tpu_custom_call" | custom-call | flops 1358954496 | bytes 2359360 | tf_op jit(solution)/shard_map/attend/pallas_call | solution.py:62
  44.8 5.7 %collective-permute-done.12.mate_ref = bf16[144,768]{1,0:T(8,128)(2,1)S(1)} collective-permute-done((bf16[144,768]{1,0:T(8,128)(2,1)S(1)}, bf16[144,768]{1,0:T(8,128)(2,1)S(1)}, u32[]{:S(2)}, u32[]{:S(2)}) %collective-permute-start.12) | collective-permute-done | bytes 221216 | tf_op jit(solution)/shard_map/ppermute | solution.py:33
  50.7 1.6 %collective-permute-start.16 = (bf16[144,384]{1,0:T(8,128)(2,1)S(1)}, bf16[144,384]{1,0:T(8,128)(2,1)S(1)}, u32[]{:S(2)}, u32[]{:S(2)}) collective-permute-start(bf16[144,384]{1,0:T(8,128)(2,1)S(1)} %pad_maximum_fusion.7), channel_id=1, source_target_pairs={{0,2},{1,3},{2,0},{3,1},{4,6},{5,7},{6,4},{7,5},{8,10},{9,11},{10,... | collective-permute-start | bytes 331784 | tf_op jit(solution)/shard_map/ppermute | solution.py:33
  52.4 1.6 %collective-permute-start.17 = (bf16[144,384]{1,0:T(8,128)(2,1)S(1)}, bf16[144,384]{1,0:T(8,128)(2,1)S(1)}, u32[]{:S(2)}, u32[]{:S(2)}) collective-permute-start(bf16[144,384]{1,0:T(8,128)(2,1)S(1)} %pad_maximum_fusion.8), channel_id=1, source_target_pairs={{0,4},{1,5},{2,6},{3,7},{4,0},{5,1},{6,2},{7,3},{8,12},{9,13},{10,... | collective-permute-start | bytes 331784 | tf_op jit(solution)/shard_map/ppermute | solution.py:33
  54.6 3.9 %collective-permute-done.15.refs_0_ = bf16[416,1152]{1,0:T(8,128)(2,1)S(1)} collective-permute-done((bf16[416,1152]{1,0:T(8,128)(2,1)S(1)}, bf16[416,1152]{1,0:T(8,128)(2,1)S(1)}, u32[]{:S(2)}, u32[]{:S(2)}) %collective-permute-start.15) | collective-permute-done | bytes 958496 | tf_op jit(solution)/shard_map/ppermute | solution.py:33
  58.5 2.3 %collective-permute-done.17.refs_9_ = bf16[144,384]{1,0:T(8,128)(2,1)S(1)} collective-permute-done((bf16[144,384]{1,0:T(8,128)(2,1)S(1)}, bf16[144,384]{1,0:T(8,128)(2,1)S(1)}, u32[]{:S(2)}, u32[]{:S(2)}) %collective-permute-start.17) | collective-permute-done | bytes 110624 | tf_op jit(solution)/shard_map/ppermute | solution.py:33
  62.7 1.9 %project.1 = (f32[192,1152]{1,0:T(8,128)S(1)}, bf16[192,1152]{1,0:T(8,128)(2,1)S(1)}) custom-call(f32[2,8,1152]{2,1,0:T(8,128)S(1)} %bitcast.35, bf16[192,1152]{1,0:T(8,128)(2,1)S(1)} %copy-done.4, bf16[144,768]{1,0:T(8,128)(2,1)S(1)} %get-tuple-element.46.mine_ref, bf16[144,768]{1,0:T(8,128)(2,1)S(1)} %collective-permute-done.12.mate_ref, ...), custom_call_target="tpu_custom_call" | custom-call | flops 509607936 | bytes 5713920 | tf_op jit(solution)/shard_map/project/pallas_call | solution.py:62
  65.9 7.1 %collective-permute-done.20.refs_1_ = bf16[192,1152]{1,0:T(8,128)(2,1)S(1)} collective-permute-done((bf16[192,1152]{1,0:T(8,128)(2,1)S(1)}, bf16[192,1152]{1,0:T(8,128)(2,1)S(1)}, u32[]{:S(2)}, u32[]{:S(2)}) %collective-permute-start.20) | collective-permute-done | bytes 442400 | tf_op jit(solution)/shard_map/ppermute | solution.py:33
  77.9 2.1 %collective-permute-done.23.refs_0_ = bf16[128,1152]{1,0:T(8,128)(2,1)S(1)} collective-permute-done((bf16[128,1152]{1,0:T(8,128)(2,1)S(1)}, bf16[128,1152]{1,0:T(8,128)(2,1)S(1)}, u32[]{:S(2)}, u32[]{:S(2)}) %collective-permute-start.23) | collective-permute-done | bytes 294944 | tf_op jit(solution)/shard_map/ppermute | solution.py:33
  89.1 2.7 %mlp_near.1 = (f32[192,1152]{1,0:T(8,128)S(1)}, f32[64,1152]{1,0:T(8,128)S(1)}, f32[64,1152]{1,0:T(8,128)S(1)}, f32[64,1152]{1,0:T(8,128)S(1)}) custom-call(bf16[1152,1152]{1,0:T(8,128)(2,1)S(1)} %get-tuple-element.60.up_ref, bf16[1152,1152]{1,0:T(8,128)(2,1)S(1)} %get-tuple-element.61.down_ref, bf16[192,1152]{1,0:T(8,128)(2,1)S(1)} %get-tuple-element.62.refs_0_, ...), custom_call_target="tpu_custom_call" | custom-call | flops 2038431744 | bytes 6193152 | tf_op jit(solution)/shard_map/mlp_near/pallas_call | solution.py:62
  94.1 3.7 %collective-permute-done.28.refs_2_ = bf16[128,1152]{1,0:T(8,128)(2,1)S(1)} collective-permute-done((bf16[128,1152]{1,0:T(8,128)(2,1)S(1)}, bf16[128,1152]{1,0:T(8,128)(2,1)S(1)}, u32[]{:S(2)}, u32[]{:S(2)}) %collective-permute-start.28) | collective-permute-done | bytes 294944 | tf_op jit(solution)/shard_map/ppermute | solution.py:33
  99.3 3.7 %collective-permute-done.31.refs_5_ = bf16[64,1152]{1,0:T(8,128)(2,1)S(1)} collective-permute-done((bf16[64,1152]{1,0:T(8,128)(2,1)S(1)}, bf16[64,1152]{1,0:T(8,128)(2,1)S(1)}, u32[]{:S(2)}, u32[]{:S(2)}) %collective-permute-start.31) | collective-permute-done | bytes 147488 | tf_op jit(solution)/shard_map/ppermute | solution.py:33
  103.1 1.9 %finish.1 = (bf16[192,1152]{1,0:T(8,128)(2,1)}, f32[16,192]{1,0:T(8,128)S(1)}, f32[16,192]{1,0:T(8,128)S(1)}) custom-call(s32[2,8]{1,0:T(2,128)S(1)} %copy-done.7, f32[2]{0:T(128)S(1)} %copy-done.9, f32[2,2]{1,0:T(2,128)S(1)} %copy-done.8, f32[2,8,1152]{2,1,0:T(8,128)S(1)} %bitcast.36, f32[192,1152]{1,0:T(8,128)S(1)} %get-tuple-element.54.mid_ref, ...), custom_call_target="tpu_custom_call" | custom-call | flops 7077888 | bytes 3219544 | tf_op jit(solution)/shard_map/finish/pallas_call | solution.py:62
  (102 shorter events, 32.6 us)
Async XLA Ops:
  1.6 10.0 %collective-permute-start.2 = (bf16[32,1152]{1,0:T(8,128)(2,1)S(1)}, bf16[32,1152]{1,0:T(8,128)(2,1)S(1)}, u32[]{:S(2)}, u32[]{:S(2)}) collective-permute-start(bf16[32,1152]{1,0:T(8,128)(2,1)S(1)} %slice.97), channel_id=1, source_target_pairs={{0,4},{1,5},{2,6},{3,7},{4,0},{5,1},{6,2},{7,3},{8,12},{9,13},{10,... | collective-permute-start | bytes 221192 | tf_op jit(solution)/shard_map/ppermute | solution.py:33
  4.7 5.2 %collective-permute-start = (bf16[64,1152]{1,0:T(8,128)(2,1)S(1)}, bf16[64,1152]{1,0:T(8,128)(2,1)S(1)}, u32[]{:S(2)}, u32[]{:S(2)}) collective-permute-start(bf16[64,1152]{1,0:T(8,128)(2,1)S(1)} %get-tuple-element.86), channel_id=1, source_target_pairs={{0,1},{1,0},{2,3},{3,2},{4,5},{5,4},{6,7},{7,6},{8,9},{9,8},{10,11... | collective-permute-start | bytes 442376 | tf_op jit(solution)/shard_map/ppermute | solution.py:33
  10.0 8.6 %collective-permute-start.1 = (bf16[200,1152]{1,0:T(8,128)(2,1)S(1)}, bf16[200,1152]{1,0:T(8,128)(2,1)S(1)}, u32[]{:S(2)}, u32[]{:S(2)}) collective-permute-start(bf16[200,1152]{1,0:T(8,128)(2,1)S(1)} %pad_maximum_fusion.1), channel_id=1, source_target_pairs={{0,2},{1,3},{2,0},{3,1},{4,6},{5,7},{6,4},{7,5},{8,10},{9,11},{10,... | collective-permute-start | bytes 1382408 | tf_op jit(solution)/shard_map/ppermute | solution.py:33
  13.1 6.4 %collective-permute-start.8 = (bf16[32,1152]{1,0:T(8,128)(2,1)S(1)}, bf16[32,1152]{1,0:T(8,128)(2,1)S(1)}, u32[]{:S(2)}, u32[]{:S(2)}) collective-permute-start(bf16[32,1152]{1,0:T(8,128)(2,1)S(1)} %collective-permute-done.2.refs_3_), channel_id=1, source_target_pairs={{0,16},{16,0},{1,17},{17,1},{2,18},{18,2},{3,19},{19,3},{4,20},{20... | collective-permute-start | bytes 221192 | tf_op jit(solution)/shard_map/ppermute | solution.py:37
  18.6 13.5 %collective-permute-start.4 = (bf16[400,1152]{1,0:T(8,128)(2,1)S(1)}, bf16[400,1152]{1,0:T(8,128)(2,1)S(1)}, u32[]{:S(2)}, u32[]{:S(2)}) collective-permute-start(bf16[400,1152]{1,0:T(8,128)(2,1)S(1)} %get-tuple-element.71), channel_id=1, source_target_pairs={{0,4},{1,5},{2,6},{3,7},{4,0},{5,1},{6,2},{7,3},{8,12},{9,13},{10,... | collective-permute-start | bytes 2764808 | tf_op jit(solution)/shard_map/ppermute | solution.py:33
  19.6 9.6 %collective-permute-start.5 = (bf16[128,1152]{1,0:T(8,128)(2,1)S(1)}, bf16[128,1152]{1,0:T(8,128)(2,1)S(1)}, u32[]{:S(2)}, u32[]{:S(2)}) collective-permute-start(bf16[128,1152]{1,0:T(8,128)(2,1)S(1)} %pad_maximum_fusion.2), channel_id=1, source_target_pairs={{0,2},{1,3},{2,0},{3,1},{4,6},{5,7},{6,4},{7,5},{8,10},{9,11},{10,... | collective-permute-start | bytes 884744 | tf_op jit(solution)/shard_map/ppermute | solution.py:33
  32.8 12.0 %collective-permute-start.13 = (bf16[288,1152]{1,0:T(8,128)(2,1)S(1)}, bf16[288,1152]{1,0:T(8,128)(2,1)S(1)}, u32[]{:S(2)}, u32[]{:S(2)}) collective-permute-start(bf16[288,1152]{1,0:T(8,128)(2,1)S(1)} %pad_maximum_fusion), channel_id=1, source_target_pairs={{0,1},{1,0},{2,3},{3,2},{4,5},{5,4},{6,7},{7,6},{8,9},{9,8},{10,11... | collective-permute-start | bytes 1990664 | tf_op jit(solution)/shard_map/ppermute | solution.py:33
  34.4 24.1 %collective-permute-start.15 = (bf16[416,1152]{1,0:T(8,128)(2,1)S(1)}, bf16[416,1152]{1,0:T(8,128)(2,1)S(1)}, u32[]{:S(2)}, u32[]{:S(2)}) collective-permute-start(bf16[416,1152]{1,0:T(8,128)(2,1)S(1)} %slice_select_fusion), channel_id=1, source_target_pairs={{0,4},{1,5},{2,6},{3,7},{4,0},{5,1},{6,2},{7,3},{8,12},{9,13},{10,... | collective-permute-start | bytes 2875400 | tf_op jit(solution)/shard_map/ppermute | solution.py:33
  44.5 6.0 %collective-permute-start.12 = (bf16[144,768]{1,0:T(8,128)(2,1)S(1)}, bf16[144,768]{1,0:T(8,128)(2,1)S(1)}, u32[]{:S(2)}, u32[]{:S(2)}) collective-permute-start(bf16[144,768]{1,0:T(8,128)(2,1)S(1)} %get-tuple-element.47), channel_id=1, source_target_pairs={{0,1},{1,0},{2,3},{3,2},{4,5},{5,4},{6,7},{7,6},{8,9},{9,8},{10,11... | collective-permute-start | bytes 663560 | tf_op jit(solution)/shard_map/ppermute | solution.py:33
  50.5 12.3 %collective-permute-start.14 = (bf16[288,1152]{1,0:T(8,128)(2,1)S(1)}, bf16[288,1152]{1,0:T(8,128)(2,1)S(1)}, u32[]{:S(2)}, u32[]{:S(2)}) collective-permute-start(bf16[288,1152]{1,0:T(8,128)(2,1)S(1)} %collective-permute-done.13.refs_3_), channel_id=1, source_target_pairs={{0,16},{16,0},{1,17},{17,1},{2,18},{18,2},{3,19},{19,3},{4,20},{20... | collective-permute-start | bytes 1990664 | tf_op jit(solution)/shard_map/ppermute | solution.py:37
  50.7 7.8 %collective-permute-start.16 = (bf16[144,384]{1,0:T(8,128)(2,1)S(1)}, bf16[144,384]{1,0:T(8,128)(2,1)S(1)}, u32[]{:S(2)}, u32[]{:S(2)}) collective-permute-start(bf16[144,384]{1,0:T(8,128)(2,1)S(1)} %pad_maximum_fusion.7), channel_id=1, source_target_pairs={{0,2},{1,3},{2,0},{3,1},{4,6},{5,7},{6,4},{7,5},{8,10},{9,11},{10,... | collective-permute-start | bytes 331784 | tf_op jit(solution)/shard_map/ppermute | solution.py:33
  52.4 8.5 %collective-permute-start.17 = (bf16[144,384]{1,0:T(8,128)(2,1)S(1)}, bf16[144,384]{1,0:T(8,128)(2,1)S(1)}, u32[]{:S(2)}, u32[]{:S(2)}) collective-permute-start(bf16[144,384]{1,0:T(8,128)(2,1)S(1)} %pad_maximum_fusion.8), channel_id=1, source_target_pairs={{0,4},{1,5},{2,6},{3,7},{4,0},{5,1},{6,2},{7,3},{8,12},{9,13},{10,... | collective-permute-start | bytes 331784 | tf_op jit(solution)/shard_map/ppermute | solution.py:33
  54.1 7.8 %collective-permute-start.18 = (bf16[144,384]{1,0:T(8,128)(2,1)S(1)}, bf16[144,384]{1,0:T(8,128)(2,1)S(1)}, u32[]{:S(2)}, u32[]{:S(2)}) collective-permute-start(bf16[144,384]{1,0:T(8,128)(2,1)S(1)} %pad_maximum_fusion.9), channel_id=1, source_target_pairs={{0,6},{1,7},{2,4},{3,5},{4,2},{5,3},{6,0},{7,1},{8,14},{9,15},{10,... | collective-permute-start | bytes 331784 | tf_op jit(solution)/shard_map/ppermute | solution.py:33
  61.9 11.2 %collective-permute-start.19 = (bf16[160,1152]{1,0:T(8,128)(2,1)S(1)}, bf16[160,1152]{1,0:T(8,128)(2,1)S(1)}, u32[]{:S(2)}, u32[]{:S(2)}) collective-permute-start(bf16[160,1152]{1,0:T(8,128)(2,1)S(1)} %slice_select_fusion.1), channel_id=1, source_target_pairs={{0,4},{1,5},{2,6},{3,7},{4,0},{5,1},{6,2},{7,3},{8,12},{9,13},{10,... | collective-permute-start | bytes 1105928 | tf_op jit(solution)/shard_map/ppermute | solution.py:33
  62.2 14.3 %collective-permute-start.21 = (bf16[416,1152]{1,0:T(8,128)(2,1)S(1)}, bf16[416,1152]{1,0:T(8,128)(2,1)S(1)}, u32[]{:S(2)}, u32[]{:S(2)}) collective-permute-start(bf16[416,1152]{1,0:T(8,128)(2,1)S(1)} %collective-permute-done.15.refs_0_), channel_id=1, source_target_pairs={{0,16},{16,0},{1,17},{17,1},{2,18},{18,2},{3,19},{19,3},{4,20},{20... | collective-permute-start | bytes 2875400 | tf_op jit(solution)/shard_map/ppermute | solution.py:37
  64.7 8.4 %collective-permute-start.20 = (bf16[192,1152]{1,0:T(8,128)(2,1)S(1)}, bf16[192,1152]{1,0:T(8,128)(2,1)S(1)}, u32[]{:S(2)}, u32[]{:S(2)}) collective-permute-start(bf16[192,1152]{1,0:T(8,128)(2,1)S(1)} %get-tuple-element.62.refs_0_), channel_id=1, source_target_pairs={{0,1},{1,0},{2,3},{3,2},{4,5},{5,4},{6,7},{7,6},{8,9},{9,8},{10,11... | collective-permute-start | bytes 1327112 | tf_op jit(solution)/shard_map/ppermute | solution.py:33
  73.3 6.8 %collective-permute-start.23 = (bf16[128,1152]{1,0:T(8,128)(2,1)S(1)}, bf16[128,1152]{1,0:T(8,128)(2,1)S(1)}, u32[]{:S(2)}, u32[]{:S(2)}) collective-permute-start(bf16[128,1152]{1,0:T(8,128)(2,1)S(1)} %pad_maximum_fusion.3), channel_id=1, source_target_pairs={{0,2},{1,3},{2,0},{3,1},{4,6},{5,7},{6,4},{7,5},{8,10},{9,11},{10,... | collective-permute-start | bytes 884744 | tf_op jit(solution)/shard_map/ppermute | solution.py:33
  74.5 8.7 %collective-permute-start.24 = (bf16[128,1152]{1,0:T(8,128)(2,1)S(1)}, bf16[128,1152]{1,0:T(8,128)(2,1)S(1)}, u32[]{:S(2)}, u32[]{:S(2)}) collective-permute-start(bf16[128,1152]{1,0:T(8,128)(2,1)S(1)} %pad_maximum_fusion.4), channel_id=1, source_target_pairs={{0,2},{1,3},{2,0},{3,1},{4,6},{5,7},{6,4},{7,5},{8,10},{9,11},{10,... | collective-permute-start | bytes 884744 | tf_op jit(solution)/shard_map/ppermute | solution.py:33
  75.4 11.0 %collective-permute-start.25 = (bf16[128,1152]{1,0:T(8,128)(2,1)S(1)}, bf16[128,1152]{1,0:T(8,128)(2,1)S(1)}, u32[]{:S(2)}, u32[]{:S(2)}) collective-permute-start(bf16[128,1152]{1,0:T(8,128)(2,1)S(1)} %pad_maximum_fusion.5), channel_id=1, source_target_pairs={{0,2},{1,3},{2,0},{3,1},{4,6},{5,7},{6,4},{7,5},{8,10},{9,11},{10,... | collective-permute-start | bytes 884744 | tf_op jit(solution)/shard_map/ppermute | solution.py:33
  81.5 10.3 %collective-permute-start.26 = (bf16[128,1152]{1,0:T(8,128)(2,1)S(1)}, bf16[128,1152]{1,0:T(8,128)(2,1)S(1)}, u32[]{:S(2)}, u32[]{:S(2)}) collective-permute-start(bf16[128,1152]{1,0:T(8,128)(2,1)S(1)} %mlp_far0.1), channel_id=1, source_target_pairs={{0,2},{1,3},{2,0},{3,1},{4,6},{5,7},{6,4},{7,5},{8,10},{9,11},{10,... | collective-permute-start | bytes 884744 | tf_op jit(solution)/shard_map/ppermute | solution.py:33
  84.7 8.4 %collective-permute-start.27 = (bf16[128,1152]{1,0:T(8,128)(2,1)S(1)}, bf16[128,1152]{1,0:T(8,128)(2,1)S(1)}, u32[]{:S(2)}, u32[]{:S(2)}) collective-permute-start(bf16[128,1152]{1,0:T(8,128)(2,1)S(1)} %mlp_far1.1), channel_id=1, source_target_pairs={{0,2},{1,3},{2,0},{3,1},{4,6},{5,7},{6,4},{7,5},{8,10},{9,11},{10,... | collective-permute-start | bytes 884744 | tf_op jit(solution)/shard_map/ppermute | solution.py:33
  87.8 10.0 %collective-permute-start.28 = (bf16[128,1152]{1,0:T(8,128)(2,1)S(1)}, bf16[128,1152]{1,0:T(8,128)(2,1)S(1)}, u32[]{:S(2)}, u32[]{:S(2)}) collective-permute-start(bf16[128,1152]{1,0:T(8,128)(2,1)S(1)} %mlp_far2.1), channel_id=1, source_target_pairs={{0,2},{1,3},{2,0},{3,1},{4,6},{5,7},{6,4},{7,5},{8,10},{9,11},{10,... | collective-permute-start | bytes 884744 | tf_op jit(solution)/shard_map/ppermute | solution.py:33
  91.9 7.4 %collective-permute-start.29 = (bf16[64,1152]{1,0:T(8,128)(2,1)S(1)}, bf16[64,1152]{1,0:T(8,128)(2,1)S(1)}, u32[]{:S(2)}, u32[]{:S(2)}) collective-permute-start(bf16[64,1152]{1,0:T(8,128)(2,1)S(1)} %add_convert_fusion.2), channel_id=1, source_target_pairs={{0,1},{1,0},{2,3},{3,2},{4,5},{5,4},{6,7},{7,6},{8,9},{9,8},{10,11... | collective-permute-start | bytes 442376 | tf_op jit(solution)/shard_map/ppermute | solution.py:33
  93.2 6.2 %collective-permute-start.30 = (bf16[64,1152]{1,0:T(8,128)(2,1)S(1)}, bf16[64,1152]{1,0:T(8,128)(2,1)S(1)}, u32[]{:S(2)}, u32[]{:S(2)}) collective-permute-start(bf16[64,1152]{1,0:T(8,128)(2,1)S(1)} %add_convert_fusion.1), channel_id=1, source_target_pairs={{0,1},{1,0},{2,3},{3,2},{4,5},{5,4},{6,7},{7,6},{8,9},{9,8},{10,11... | collective-permute-start | bytes 442376 | tf_op jit(solution)/shard_map/ppermute | solution.py:33
  (19 other events, 103.9 us)

commit v3 on v2

--- a/solution.py
+++ b/solution.py
@@ -17,7 +17,7 @@
 SMALL = (4, 1, 2)
 PROJ = ((2, 4, 1), (4, 1, 2))
 HEADS_TO = ((2, 4, 1), (4, 1, 2))
-FAR_EARLY = 416
+FAR_EARLY = 384
 CHUNKS = 3
 F32 = jnp.float32
 BF16 = jnp.bfloat16
@@ -71,8 +71,16 @@
     )(*operands)
 
 
+def pad_weight(weight_ref, padded):
+    weight = weight_ref[...].astype(F32)
+    unused = jnp.zeros((LANES - HEAD_DIM, weight.shape[1]), F32)
+    for part in range(weight.shape[0] // HEAD_DIM):
+        rows = jnp.concatenate([weight[part * HEAD_DIM : (part + 1) * HEAD_DIM], unused])
+        padded[part * LANES : (part + 1) * LANES, :] = rows.astype(BF16)
+
+
 def qkv_kernel(row_counts, mod_ref, weight_ref, *refs):
-    row_refs, out_ref, normed, padded = refs[:-3], refs[-3], refs[-2], refs[-1]
+    row_refs, (out_ref, *made, normed) = refs[: len(row_counts)], refs[len(row_counts) :]
     _, latent, _ = place()
     shift, scale = mod_row(mod_ref, latent, 0), 1.0 + mod_row(mod_ref, latent, 1)
     chunk = 32
@@ -82,11 +90,10 @@
             rows = ref[low : low + chunk, :].astype(F32)
             normed[at : at + chunk, :] = (normalized(rows) * scale + shift).astype(BF16)
             at += chunk
-    weight = weight_ref[...].astype(F32)
-    unused = jnp.zeros((LANES - HEAD_DIM, weight.shape[1]), F32)
-    for part in range(weight.shape[0] // HEAD_DIM):
-        rows = jnp.concatenate([weight[part * HEAD_DIM : (part + 1) * HEAD_DIM], unused])
-        padded[part * LANES : (part + 1) * LANES, :] = rows.astype(BF16)
+    padded = weight_ref
+    if made:
+        padded = made[0]
+        pad_weight(weight_ref, padded)
     lane = lax.broadcasted_iota(jnp.int32, (1, padded.shape[0]), 1)
     width = padded.shape[0] // 3
     factor = jnp.where(lane < width, HEAD_DIM ** (-0.5) * math.log2(math.e), 1.0)
@@ -99,15 +106,18 @@
         out_ref[low : low + block, :] = (out * factor + ones).astype(BF16)
 
 
-def qkv_rows(modulation, weight, pieces, row_counts, name):
-    count = sum(row_counts)
-    parts, width = weight.shape[0] // HEAD_DIM, weight.shape[1]
+def qkv_rows(modulation, weight, pieces, row_counts, make_padded, name):
+    count, width = sum(row_counts), weight.shape[1]
+    padded_rows = weight.shape[0] // HEAD_DIM * LANES if make_padded else weight.shape[0]
+    outs = [jax.ShapeDtypeStruct((count, padded_rows), BF16)]
+    if make_padded:
+        outs.append(jax.ShapeDtypeStruct((padded_rows, width), BF16))
     return call(
         functools.partial(qkv_kernel, row_counts),
-        jax.ShapeDtypeStruct((count, parts * LANES), BF16),
+        tuple(outs),
         (modulation, weight) + tuple(pieces),
-        scratch=[pltpu.VMEM((count, width), BF16), pltpu.VMEM((parts * LANES, width), BF16)],
-        flops=2 * count * width * parts * LANES,
+        scratch=[pltpu.VMEM((count, width), BF16)],
+        flops=2 * count * width * padded_rows,
         name=name,
     )
 
@@ -425,15 +435,15 @@
             ]
             proj_rows = proj_own[0]
         elif step == 1:
-            got_large, got_small = lax.optimization_barrier((got_large, got_small))
             proj_rows = jnp.concatenate([proj_rows, got_large[2 * large :]])
         else:
-            early = qkv_rows(
+            early, qkv_padded = qkv_rows(
                 modulation,
                 qkv_rows_t,
                 (hidden_in, got[0][0], got[1][0], got[0][1], got[1][1])
                 + (away[0][0], away[1][0], away[0][1], away[1][1]),
                 (cap, large, 2 * large, small, 2 * small) + (large, 2 * large, small, 2 * small),
+                True,
                 "qkv_early",
             )
             got_large, got_small, early, *sent = lax.optimization_barrier(
@@ -447,9 +457,10 @@
         away.append((from_other_half(got_large), from_other_half(got_small)))
     proj_last = permute_by(proj_rows, [order[2] for order in PROJ])
     far = [permute_by(sent[0], [GROUP // 2] * 2)]
-    late = [qkv_rows(modulation, qkv_rows_t, got[2], (4 * large, 4 * small), "qkv_late_own")]
+    counts = (4 * large, 4 * small)
+    late = list(qkv_rows(modulation, qkv_padded, got[2], counts, False, "qkv_late_own"))
     *other, late[0] = lax.optimization_barrier((*away[2], late[0]))
-    late.append(qkv_rows(modulation, qkv_rows_t, other, (4 * large, 4 * small), "qkv_late_other"))
+    late += qkv_rows(modulation, qkv_padded, other, counts, False, "qkv_late_other")
     mine, sent_heads = attention(piece_rows, early, late, cap)
     mate = permute_by(sent_heads, [order[2] for order in HEADS_TO])
     mate, proj_last = lax.optimization_barrier((mate, proj_last))

time: 107 us -> 107 us (level)
  waiting for transfers between devices: 47.8 us -> 54.6 us
  starting transfers between devices: 29.7 us -> 23.5 us
    ppermute x23, starting transfers between devices: 27.9 us -> 22.4 us  [permute_by(): return lax.ppermute(block, ('cfg', 'tok'), route)]
    ppermute x23, waiting for transfers between devices: 46.6 us -> 51.9 us  [permute_by(): return lax.ppermute(block, ('cfg', 'tok'), route)]
    ppermute x10, waiting for transfers between devices: 1.2 us -> 2.65 us  [from_other_half(): return lax.ppermute(block, 'cfg', [(0, 1), (1, 0)])]
  transfers between devices with their start and end apart: 33 -> 33, of which waited for: 16 -> 19; matrix products, arithmetic and copies ran while one was open for 2% -> 2% of each run, Pallas kernels for 21% -> 21%
where the time goes in v3:
time: 107 us
  waiting for transfers between devices  54.6 us (51%)
  Pallas kernels  24.3 us (23%)
  starting transfers between devices  23.5 us (22%)
  local copies, waits for them, and re-layouts  2.48 us (2%)
  other arithmetic  1.35 us (1%)
    ppermute x23, waiting for transfers between devices, permute_by(): return lax.ppermute(block, ('cfg', 'tok'), route)  51.9 us
    pallas_call x11, Pallas kernels, call(): pl.pallas_call(kernel, out_shape=out_shape, in_specs=specs or [whole] * l...  24.3 us
    ppermute x23, starting transfers between devices, permute_by(): return lax.ppermute(block, ('cfg', 'tok'), route)  22.4 us
    ppermute x10, waiting for transfers between devices, from_other_half(): return lax.ppermute(block, 'cfg', [(0, 1), (1, 0)])  2.65 us
  transfers between devices with their start and end apart: 33, of which 19 were waited for; matrix products, arithmetic and copies ran while one was open for 2% of the time, Pallas kernels for 21%

profile of v3, /device:TPU:0, one launch (start us, length us, event | category | flops | bytes accessed | tf_op | source)
XLA Modules:
  0.0 107.3 jit_solution(11799345562973228175)
XLA Ops:
  1.6 3.1 %collective-permute-start.3 = (bf16[32,1152]{1,0:T(8,128)(2,1)S(1)}, bf16[32,1152]{1,0:T(8,128)(2,1)S(1)}, u32[]{:S(2)}, u32[]{:S(2)}) collective-permute-start(bf16[32,1152]{1,0:T(8,128)(2,1)S(1)} %slice.99), channel_id=1, source_target_pairs={{0,4},{1,5},{2,6},{3,7},{4,0},{5,1},{6,2},{7,3},{8,12},{9,13},{10,... | collective-permute-start | bytes 221192 | tf_op jit(solution)/shard_map/ppermute | solution.py:33
  7.3 2.6 %collective-permute-done.refs_1_ = bf16[64,1152]{1,0:T(8,128)(2,1)S(1)} collective-permute-done((bf16[64,1152]{1,0:T(8,128)(2,1)S(1)}, bf16[64,1152]{1,0:T(8,128)(2,1)S(1)}, u32[]{:S(2)}, u32[]{:S(2)}) %collective-permute-start) | collective-permute-done | bytes 147488 | tf_op jit(solution)/shard_map/ppermute | solution.py:33
  10.0 1.6 %collective-permute-start.1 = (bf16[200,1152]{1,0:T(8,128)(2,1)S(1)}, bf16[200,1152]{1,0:T(8,128)(2,1)S(1)}, u32[]{:S(2)}, u32[]{:S(2)}) collective-permute-start(bf16[200,1152]{1,0:T(8,128)(2,1)S(1)} %pad_maximum_fusion.1), channel_id=1, source_target_pairs={{0,2},{1,3},{2,0},{3,1},{4,6},{5,7},{6,4},{7,5},{8,10},{9,11},{10,... | collective-permute-start | bytes 1382408 | tf_op jit(solution)/shard_map/ppermute | solution.py:33
  13.2 5.4 %collective-permute-done.1.refs_2_.refs_1_ = bf16[200,1152]{1,0:T(8,128)(2,1)S(1)} collective-permute-done((bf16[200,1152]{1,0:T(8,128)(2,1)S(1)}, bf16[200,1152]{1,0:T(8,128)(2,1)S(1)}, u32[]{:S(2)}, u32[]{:S(2)}) %collective-permute-start.1) | collective-permute-done | bytes 460832 | tf_op jit(solution)/shard_map/ppermute | solution.py:33
  19.0 2.0 %collective-permute-start.5 = (bf16[128,1152]{1,0:T(8,128)(2,1)S(1)}, bf16[128,1152]{1,0:T(8,128)(2,1)S(1)}, u32[]{:S(2)}, u32[]{:S(2)}) collective-permute-start(bf16[128,1152]{1,0:T(8,128)(2,1)S(1)} %pad_maximum_fusion.2), channel_id=1, source_target_pairs={{0,2},{1,3},{2,0},{3,1},{4,6},{5,7},{6,4},{7,5},{8,10},{9,11},{10,... | collective-permute-start | bytes 884744 | tf_op jit(solution)/shard_map/ppermute | solution.py:33
  23.1 2.5 %qkv_early.1 = (bf16[768,768]{1,0:T(8,128)(2,1)S(1)}, bf16[768,1152]{1,0:T(8,128)(2,1)S(1)}) custom-call(f32[2,8,1152]{2,1,0:T(8,128)S(1)} %bitcast.29, bf16[432,1152]{1,0:T(8,128)(2,1)S(1)} %bitcast.36, bf16[192,1152]{1,0:T(8,128)(2,1)S(1)} %copy-done.3, bf16[64,1152]{1,0:T(8,128)(2,1)S(1)} %collective-permute-done.refs_1_, ...), custom_call_target="tpu_custom_call" | custom-call | flops 1358954496 | bytes 3170304 | tf_op jit(solution)/shard_map/qkv_early/pallas_call | solution.py:62
  25.6 3.1 %collective-permute-done.5.refs_1_ = bf16[128,1152]{1,0:T(8,128)(2,1)S(1)} collective-permute-done((bf16[128,1152]{1,0:T(8,128)(2,1)S(1)}, bf16[128,1152]{1,0:T(8,128)(2,1)S(1)}, u32[]{:S(2)}, u32[]{:S(2)}) %collective-permute-start.5) | collective-permute-done | bytes 294944 | tf_op jit(solution)/shard_map/ppermute | solution.py:33
  28.7 3.5 %collective-permute-done.2.refs_0_.refs_2_ = bf16[400,1152]{1,0:T(8,128)(2,1)S(1)} collective-permute-done((bf16[400,1152]{1,0:T(8,128)(2,1)S(1)}, bf16[400,1152]{1,0:T(8,128)(2,1)S(1)}, u32[]{:S(2)}, u32[]{:S(2)}) %collective-permute-start.2) | collective-permute-done | bytes 921632 | tf_op jit(solution)/shard_map/ppermute | solution.py:33
  34.8 1.6 %qkv_late_own.1.refs_0_ = bf16[384,768]{1,0:T(8,128)(2,1)S(1)} custom-call(f32[2,8,1152]{2,1,0:T(8,128)S(1)} %bitcast.30, bf16[768,1152]{1,0:T(8,128)(2,1)S(1)} %get-tuple-element.42.weight_ref, bf16[400,1152]{1,0:T(8,128)(2,1)S(1)} %collective-permute-done.2.refs_0_.refs_2_, bf16[128,1152]{1,0:T(8,128)(2,1)S(1)} %collective-permute-done.5.refs_1_), custom_call_target="tpu_custom_call" | custom-call | flops 679477248 | bytes 3059712 | tf_op jit(solution)/shard_map/qkv_late_own/pallas_call | solution.py:62
  36.5 1.6 %qkv_late_other.1.refs_1_ = bf16[384,768]{1,0:T(8,128)(2,1)S(1)} custom-call(f32[2,8,1152]{2,1,0:T(8,128)S(1)} %bitcast.31, bf16[768,1152]{1,0:T(8,128)(2,1)S(1)} %get-tuple-element.42.weight_ref, bf16[400,1152]{1,0:T(8,128)(2,1)S(1)} %collective-permute-done.10.refs_0_.refs_6_, bf16[128,1152]{1,0:T(8,128)(2,1)S(1)} %collective-permute-done.11.refs_1_), custom_call_target="tpu_custom_call" | custom-call | flops 679477248 | bytes 3059712 | tf_op jit(solution)/shard_map/qkv_late_other/pallas_call | solution.py:62
  38.1 6.2 %attend.1 = (bf16[144,768]{1,0:T(8,128)(2,1)S(1)}, bf16[144,768]{1,0:T(8,128)(2,1)S(1)}) custom-call(s32[2,8]{1,0:T(2,128)S(1)} %copy-done.6, bf16[768,768]{1,0:T(8,128)(2,1)S(1)} %get-tuple-element.39.early_ref, bf16[384,768]{1,0:T(8,128)(2,1)S(1)} %qkv_late_own.1.refs_0_, bf16[384,768]{1,0:T(8,128)(2,1)S(1)} %qkv_late_other.1.refs_1_), custom_call_target="tpu_custom_call" | custom-call | flops 1358954496 | bytes 2359360 | tf_op jit(solution)/shard_map/attend/pallas_call | solution.py:62
  44.6 5.7 %collective-permute-done.12.mate_ref = bf16[144,768]{1,0:T(8,128)(2,1)S(1)} collective-permute-done((bf16[144,768]{1,0:T(8,128)(2,1)S(1)}, bf16[144,768]{1,0:T(8,128)(2,1)S(1)}, u32[]{:S(2)}, u32[]{:S(2)}) %collective-permute-start.12) | collective-permute-done | bytes 221216 | tf_op jit(solution)/shard_map/ppermute | solution.py:33
  52.2 1.7 %collective-permute-start.17 = (bf16[144,384]{1,0:T(8,128)(2,1)S(1)}, bf16[144,384]{1,0:T(8,128)(2,1)S(1)}, u32[]{:S(2)}, u32[]{:S(2)}) collective-permute-start(bf16[144,384]{1,0:T(8,128)(2,1)S(1)} %pad_maximum_fusion.8), channel_id=1, source_target_pairs={{0,4},{1,5},{2,6},{3,7},{4,0},{5,1},{6,2},{7,3},{8,12},{9,13},{10,... | collective-permute-start | bytes 331784 | tf_op jit(solution)/shard_map/ppermute | solution.py:33
  54.4 2.5 %collective-permute-done.15.refs_0_ = bf16[384,1152]{1,0:T(8,128)(2,1)S(1)} collective-permute-done((bf16[384,1152]{1,0:T(8,128)(2,1)S(1)}, bf16[384,1152]{1,0:T(8,128)(2,1)S(1)}, u32[]{:S(2)}, u32[]{:S(2)}) %collective-permute-start.15) | collective-permute-done | bytes 884768 | tf_op jit(solution)/shard_map/ppermute | solution.py:33
  56.9 2.3 %collective-permute-done.17.refs_9_ = bf16[144,384]{1,0:T(8,128)(2,1)S(1)} collective-permute-done((bf16[144,384]{1,0:T(8,128)(2,1)S(1)}, bf16[144,384]{1,0:T(8,128)(2,1)S(1)}, u32[]{:S(2)}, u32[]{:S(2)}) %collective-permute-start.17) | collective-permute-done | bytes 110624 | tf_op jit(solution)/shard_map/ppermute | solution.py:33
  61.0 1.9 %project.1 = (f32[192,1152]{1,0:T(8,128)S(1)}, bf16[192,1152]{1,0:T(8,128)(2,1)S(1)}) custom-call(f32[2,8,1152]{2,1,0:T(8,128)S(1)} %bitcast.32, bf16[192,1152]{1,0:T(8,128)(2,1)S(1)} %copy-done.3, bf16[144,768]{1,0:T(8,128)(2,1)S(1)} %get-tuple-element.46.mine_ref, bf16[144,768]{1,0:T(8,128)(2,1)S(1)} %collective-permute-done.12.mate_ref, ...), custom_call_target="tpu_custom_call" | custom-call | flops 509607936 | bytes 5713920 | tf_op jit(solution)/shard_map/project/pallas_call | solution.py:62
  64.3 6.9 %collective-permute-done.20.refs_1_ = bf16[192,1152]{1,0:T(8,128)(2,1)S(1)} collective-permute-done((bf16[192,1152]{1,0:T(8,128)(2,1)S(1)}, bf16[192,1152]{1,0:T(8,128)(2,1)S(1)}, u32[]{:S(2)}, u32[]{:S(2)}) %collective-permute-start.20) | collective-permute-done | bytes 442400 | tf_op jit(solution)/shard_map/ppermute | solution.py:33
  73.0 2.0 %collective-permute-start.24 = (bf16[128,1152]{1,0:T(8,128)(2,1)S(1)}, bf16[128,1152]{1,0:T(8,128)(2,1)S(1)}, u32[]{:S(2)}, u32[]{:S(2)}) collective-permute-start(bf16[128,1152]{1,0:T(8,128)(2,1)S(1)} %pad_maximum_fusion.4), channel_id=1, source_target_pairs={{0,2},{1,3},{2,0},{3,1},{4,6},{5,7},{6,4},{7,5},{8,10},{9,11},{10,... | collective-permute-start | bytes 884744 | tf_op jit(solution)/shard_map/ppermute | solution.py:33
  76.5 3.3 %collective-permute-done.23.refs_0_ = bf16[128,1152]{1,0:T(8,128)(2,1)S(1)} collective-permute-done((bf16[128,1152]{1,0:T(8,128)(2,1)S(1)}, bf16[128,1152]{1,0:T(8,128)(2,1)S(1)}, u32[]{:S(2)}, u32[]{:S(2)}) %collective-permute-start.23) | collective-permute-done | bytes 294944 | tf_op jit(solution)/shard_map/ppermute | solution.py:33
  81.3 1.6 %collective-permute-done.24.refs_0_ = bf16[128,1152]{1,0:T(8,128)(2,1)S(1)} collective-permute-done((bf16[128,1152]{1,0:T(8,128)(2,1)S(1)}, bf16[128,1152]{1,0:T(8,128)(2,1)S(1)}, u32[]{:S(2)}, u32[]{:S(2)}) %collective-permute-start.24) | collective-permute-done | bytes 294944 | tf_op jit(solution)/shard_map/ppermute | solution.py:33
  88.0 2.7 %mlp_near.1 = (f32[192,1152]{1,0:T(8,128)S(1)}, f32[64,1152]{1,0:T(8,128)S(1)}, f32[64,1152]{1,0:T(8,128)S(1)}, f32[64,1152]{1,0:T(8,128)S(1)}) custom-call(bf16[1152,1152]{1,0:T(8,128)(2,1)S(1)} %get-tuple-element.60.up_ref, bf16[1152,1152]{1,0:T(8,128)(2,1)S(1)} %get-tuple-element.61.down_ref, bf16[192,1152]{1,0:T(8,128)(2,1)S(1)} %get-tuple-element.62.refs_0_, ...), custom_call_target="tpu_custom_call" | custom-call | flops 2038431744 | bytes 6193152 | tf_op jit(solution)/shard_map/mlp_near/pallas_call | solution.py:62
  93.0 5.3 %collective-permute-done.28.refs_2_ = bf16[128,1152]{1,0:T(8,128)(2,1)S(1)} collective-permute-done((bf16[128,1152]{1,0:T(8,128)(2,1)S(1)}, bf16[128,1152]{1,0:T(8,128)(2,1)S(1)}, u32[]{:S(2)}, u32[]{:S(2)}) %collective-permute-start.28) | collective-permute-done | bytes 294944 | tf_op jit(solution)/shard_map/ppermute | solution.py:33
  98.4 5.1 %collective-permute-done.31.refs_5_ = bf16[64,1152]{1,0:T(8,128)(2,1)S(1)} collective-permute-done((bf16[64,1152]{1,0:T(8,128)(2,1)S(1)}, bf16[64,1152]{1,0:T(8,128)(2,1)S(1)}, u32[]{:S(2)}, u32[]{:S(2)}) %collective-permute-start.31) | collective-permute-done | bytes 147488 | tf_op jit(solution)/shard_map/ppermute | solution.py:33
  103.5 2.0 %finish.1 = (bf16[192,1152]{1,0:T(8,128)(2,1)}, f32[16,192]{1,0:T(8,128)S(1)}, f32[16,192]{1,0:T(8,128)S(1)}) custom-call(s32[2,8]{1,0:T(2,128)S(1)} %copy-done.6, f32[2]{0:T(128)S(1)} %copy-done.8, f32[2,2]{1,0:T(2,128)S(1)} %copy-done.7, f32[2,8,1152]{2,1,0:T(8,128)S(1)} %bitcast.33, f32[192,1152]{1,0:T(8,128)S(1)} %get-tuple-element.54.mid_ref, ...), custom_call_target="tpu_custom_call" | custom-call | flops 7077888 | bytes 3219544 | tf_op jit(solution)/shard_map/finish/pallas_call | solution.py:62
  (102 shorter events, 30.0 us)
Async XLA Ops:
  1.6 10.0 %collective-permute-start.3 = (bf16[32,1152]{1,0:T(8,128)(2,1)S(1)}, bf16[32,1152]{1,0:T(8,128)(2,1)S(1)}, u32[]{:S(2)}, u32[]{:S(2)}) collective-permute-start(bf16[32,1152]{1,0:T(8,128)(2,1)S(1)} %slice.99), channel_id=1, source_target_pairs={{0,4},{1,5},{2,6},{3,7},{4,0},{5,1},{6,2},{7,3},{8,12},{9,13},{10,... | collective-permute-start | bytes 221192 | tf_op jit(solution)/shard_map/ppermute | solution.py:33
  10.0 8.6 %collective-permute-start.1 = (bf16[200,1152]{1,0:T(8,128)(2,1)S(1)}, bf16[200,1152]{1,0:T(8,128)(2,1)S(1)}, u32[]{:S(2)}, u32[]{:S(2)}) collective-permute-start(bf16[200,1152]{1,0:T(8,128)(2,1)S(1)} %pad_maximum_fusion.1), channel_id=1, source_target_pairs={{0,2},{1,3},{2,0},{3,1},{4,6},{5,7},{6,4},{7,5},{8,10},{9,11},{10,... | collective-permute-start | bytes 1382408 | tf_op jit(solution)/shard_map/ppermute | solution.py:33
  11.6 7.4 %collective-permute-start.4 = (bf16[64,1152]{1,0:T(8,128)(2,1)S(1)}, bf16[64,1152]{1,0:T(8,128)(2,1)S(1)}, u32[]{:S(2)}, u32[]{:S(2)}) collective-permute-start(bf16[64,1152]{1,0:T(8,128)(2,1)S(1)} %pad_maximum_fusion.6), channel_id=1, source_target_pairs={{0,1},{1,0},{2,3},{3,2},{4,5},{5,4},{6,7},{7,6},{8,9},{9,8},{10,11... | collective-permute-start | bytes 442376 | tf_op jit(solution)/shard_map/ppermute | solution.py:33
  13.1 8.1 %collective-permute-start.8 = (bf16[32,1152]{1,0:T(8,128)(2,1)S(1)}, bf16[32,1152]{1,0:T(8,128)(2,1)S(1)}, u32[]{:S(2)}, u32[]{:S(2)}) collective-permute-start(bf16[32,1152]{1,0:T(8,128)(2,1)S(1)} %collective-permute-done.3.refs_3_), channel_id=1, source_target_pairs={{0,16},{16,0},{1,17},{17,1},{2,18},{18,2},{3,19},{19,3},{4,20},{20... | collective-permute-start | bytes 221192 | tf_op jit(solution)/shard_map/ppermute | solution.py:37
  18.6 13.5 %collective-permute-start.2 = (bf16[400,1152]{1,0:T(8,128)(2,1)S(1)}, bf16[400,1152]{1,0:T(8,128)(2,1)S(1)}, u32[]{:S(2)}, u32[]{:S(2)}) collective-permute-start(bf16[400,1152]{1,0:T(8,128)(2,1)S(1)} %get-tuple-element.71), channel_id=1, source_target_pairs={{0,4},{1,5},{2,6},{3,7},{4,0},{5,1},{6,2},{7,3},{8,12},{9,13},{10,... | collective-permute-start | bytes 2764808 | tf_op jit(solution)/shard_map/ppermute | solution.py:33
  19.0 9.7 %collective-permute-start.5 = (bf16[128,1152]{1,0:T(8,128)(2,1)S(1)}, bf16[128,1152]{1,0:T(8,128)(2,1)S(1)}, u32[]{:S(2)}, u32[]{:S(2)}) collective-permute-start(bf16[128,1152]{1,0:T(8,128)(2,1)S(1)} %pad_maximum_fusion.2), channel_id=1, source_target_pairs={{0,2},{1,3},{2,0},{3,1},{4,6},{5,7},{6,4},{7,5},{8,10},{9,11},{10,... | collective-permute-start | bytes 884744 | tf_op jit(solution)/shard_map/ppermute | solution.py:33
  32.8 11.8 %collective-permute-start.13 = (bf16[288,1152]{1,0:T(8,128)(2,1)S(1)}, bf16[288,1152]{1,0:T(8,128)(2,1)S(1)}, u32[]{:S(2)}, u32[]{:S(2)}) collective-permute-start(bf16[288,1152]{1,0:T(8,128)(2,1)S(1)} %pad_maximum_fusion), channel_id=1, source_target_pairs={{0,1},{1,0},{2,3},{3,2},{4,5},{5,4},{6,7},{7,6},{8,9},{9,8},{10,11... | collective-permute-start | bytes 1990664 | tf_op jit(solution)/shard_map/ppermute | solution.py:33
  34.4 22.6 %collective-permute-start.15 = (bf16[384,1152]{1,0:T(8,128)(2,1)S(1)}, bf16[384,1152]{1,0:T(8,128)(2,1)S(1)}, u32[]{:S(2)}, u32[]{:S(2)}) collective-permute-start(bf16[384,1152]{1,0:T(8,128)(2,1)S(1)} %slice_select_fusion), channel_id=1, source_target_pairs={{0,4},{1,5},{2,6},{3,7},{4,0},{5,1},{6,2},{7,3},{8,12},{9,13},{10,... | collective-permute-start | bytes 2654216 | tf_op jit(solution)/shard_map/ppermute | solution.py:33
  44.3 6.0 %collective-permute-start.12 = (bf16[144,768]{1,0:T(8,128)(2,1)S(1)}, bf16[144,768]{1,0:T(8,128)(2,1)S(1)}, u32[]{:S(2)}, u32[]{:S(2)}) collective-permute-start(bf16[144,768]{1,0:T(8,128)(2,1)S(1)} %get-tuple-element.47), channel_id=1, source_target_pairs={{0,1},{1,0},{2,3},{3,2},{4,5},{5,4},{6,7},{7,6},{8,9},{9,8},{10,11... | collective-permute-start | bytes 663560 | tf_op jit(solution)/shard_map/ppermute | solution.py:33
  50.3 10.7 %collective-permute-start.14 = (bf16[288,1152]{1,0:T(8,128)(2,1)S(1)}, bf16[288,1152]{1,0:T(8,128)(2,1)S(1)}, u32[]{:S(2)}, u32[]{:S(2)}) collective-permute-start(bf16[288,1152]{1,0:T(8,128)(2,1)S(1)} %collective-permute-done.13.refs_3_), channel_id=1, source_target_pairs={{0,16},{16,0},{1,17},{17,1},{2,18},{18,2},{3,19},{19,3},{4,20},{20... | collective-permute-start | bytes 1990664 | tf_op jit(solution)/shard_map/ppermute | solution.py:37
  50.6 6.4 %collective-permute-start.16 = (bf16[144,384]{1,0:T(8,128)(2,1)S(1)}, bf16[144,384]{1,0:T(8,128)(2,1)S(1)}, u32[]{:S(2)}, u32[]{:S(2)}) collective-permute-start(bf16[144,384]{1,0:T(8,128)(2,1)S(1)} %pad_maximum_fusion.7), channel_id=1, source_target_pairs={{0,2},{1,3},{2,0},{3,1},{4,6},{5,7},{6,4},{7,5},{8,10},{9,11},{10,... | collective-permute-start | bytes 331784 | tf_op jit(solution)/shard_map/ppermute | solution.py:33
  52.2 7.0 %collective-permute-start.17 = (bf16[144,384]{1,0:T(8,128)(2,1)S(1)}, bf16[144,384]{1,0:T(8,128)(2,1)S(1)}, u32[]{:S(2)}, u32[]{:S(2)}) collective-permute-start(bf16[144,384]{1,0:T(8,128)(2,1)S(1)} %pad_maximum_fusion.8), channel_id=1, source_target_pairs={{0,4},{1,5},{2,6},{3,7},{4,0},{5,1},{6,2},{7,3},{8,12},{9,13},{10,... | collective-permute-start | bytes 331784 | tf_op jit(solution)/shard_map/ppermute | solution.py:33
  54.0 6.4 %collective-permute-start.18 = (bf16[144,384]{1,0:T(8,128)(2,1)S(1)}, bf16[144,384]{1,0:T(8,128)(2,1)S(1)}, u32[]{:S(2)}, u32[]{:S(2)}) collective-permute-start(bf16[144,384]{1,0:T(8,128)(2,1)S(1)} %pad_maximum_fusion.9), channel_id=1, source_target_pairs={{0,6},{1,7},{2,4},{3,5},{4,2},{5,3},{6,0},{7,1},{8,14},{9,15},{10,... | collective-permute-start | bytes 331784 | tf_op jit(solution)/shard_map/ppermute | solution.py:33
  60.4 12.6 %collective-permute-start.19 = (bf16[192,1152]{1,0:T(8,128)(2,1)S(1)}, bf16[192,1152]{1,0:T(8,128)(2,1)S(1)}, u32[]{:S(2)}, u32[]{:S(2)}) collective-permute-start(bf16[192,1152]{1,0:T(8,128)(2,1)S(1)} %slice_select_fusion.1), channel_id=1, source_target_pairs={{0,4},{1,5},{2,6},{3,7},{4,0},{5,1},{6,2},{7,3},{8,12},{9,13},{10,... | collective-permute-start | bytes 1327112 | tf_op jit(solution)/shard_map/ppermute | solution.py:33
  61.0 14.1 %collective-permute-start.21 = (bf16[384,1152]{1,0:T(8,128)(2,1)S(1)}, bf16[384,1152]{1,0:T(8,128)(2,1)S(1)}, u32[]{:S(2)}, u32[]{:S(2)}) collective-permute-start(bf16[384,1152]{1,0:T(8,128)(2,1)S(1)} %collective-permute-done.15.refs_0_), channel_id=1, source_target_pairs={{0,16},{16,0},{1,17},{17,1},{2,18},{18,2},{3,19},{19,3},{4,20},{20... | collective-permute-start | bytes 2654216 | tf_op jit(solution)/shard_map/ppermute | solution.py:37
  62.9 8.4 %collective-permute-start.20 = (bf16[192,1152]{1,0:T(8,128)(2,1)S(1)}, bf16[192,1152]{1,0:T(8,128)(2,1)S(1)}, u32[]{:S(2)}, u32[]{:S(2)}) collective-permute-start(bf16[192,1152]{1,0:T(8,128)(2,1)S(1)} %get-tuple-element.62.refs_0_), channel_id=1, source_target_pairs={{0,1},{1,0},{2,3},{3,2},{4,5},{5,4},{6,7},{7,6},{8,9},{9,8},{10,11... | collective-permute-start | bytes 1327112 | tf_op jit(solution)/shard_map/ppermute | solution.py:33
  73.0 6.7 %collective-permute-start.23 = (bf16[128,1152]{1,0:T(8,128)(2,1)S(1)}, bf16[128,1152]{1,0:T(8,128)(2,1)S(1)}, u32[]{:S(2)}, u32[]{:S(2)}) collective-permute-start(bf16[128,1152]{1,0:T(8,128)(2,1)S(1)} %pad_maximum_fusion.3), channel_id=1, source_target_pairs={{0,2},{1,3},{2,0},{3,1},{4,6},{5,7},{6,4},{7,5},{8,10},{9,11},{10,... | collective-permute-start | bytes 884744 | tf_op jit(solution)/shard_map/ppermute | solution.py:33
  73.0 9.9 %collective-permute-start.24 = (bf16[128,1152]{1,0:T(8,128)(2,1)S(1)}, bf16[128,1152]{1,0:T(8,128)(2,1)S(1)}, u32[]{:S(2)}, u32[]{:S(2)}) collective-permute-start(bf16[128,1152]{1,0:T(8,128)(2,1)S(1)} %pad_maximum_fusion.4), channel_id=1, source_target_pairs={{0,2},{1,3},{2,0},{3,1},{4,6},{5,7},{6,4},{7,5},{8,10},{9,11},{10,... | collective-permute-start | bytes 884744 | tf_op jit(solution)/shard_map/ppermute | solution.py:33
  75.0 11.0 %collective-permute-start.25 = (bf16[128,1152]{1,0:T(8,128)(2,1)S(1)}, bf16[128,1152]{1,0:T(8,128)(2,1)S(1)}, u32[]{:S(2)}, u32[]{:S(2)}) collective-permute-start(bf16[128,1152]{1,0:T(8,128)(2,1)S(1)} %pad_maximum_fusion.5), channel_id=1, source_target_pairs={{0,2},{1,3},{2,0},{3,1},{4,6},{5,7},{6,4},{7,5},{8,10},{9,11},{10,... | collective-permute-start | bytes 884744 | tf_op jit(solution)/shard_map/ppermute | solution.py:33
  81.2 9.6 %collective-permute-start.26 = (bf16[128,1152]{1,0:T(8,128)(2,1)S(1)}, bf16[128,1152]{1,0:T(8,128)(2,1)S(1)}, u32[]{:S(2)}, u32[]{:S(2)}) collective-permute-start(bf16[128,1152]{1,0:T(8,128)(2,1)S(1)} %mlp_far0.1), channel_id=1, source_target_pairs={{0,2},{1,3},{2,0},{3,1},{4,6},{5,7},{6,4},{7,5},{8,10},{9,11},{10,... | collective-permute-start | bytes 884744 | tf_op jit(solution)/shard_map/ppermute | solution.py:33
  84.3 8.0 %collective-permute-start.27 = (bf16[128,1152]{1,0:T(8,128)(2,1)S(1)}, bf16[128,1152]{1,0:T(8,128)(2,1)S(1)}, u32[]{:S(2)}, u32[]{:S(2)}) collective-permute-start(bf16[128,1152]{1,0:T(8,128)(2,1)S(1)} %mlp_far1.1), channel_id=1, source_target_pairs={{0,2},{1,3},{2,0},{3,1},{4,6},{5,7},{6,4},{7,5},{8,10},{9,11},{10,... | collective-permute-start | bytes 884744 | tf_op jit(solution)/shard_map/ppermute | solution.py:33
  87.5 10.8 %collective-permute-start.28 = (bf16[128,1152]{1,0:T(8,128)(2,1)S(1)}, bf16[128,1152]{1,0:T(8,128)(2,1)S(1)}, u32[]{:S(2)}, u32[]{:S(2)}) collective-permute-start(bf16[128,1152]{1,0:T(8,128)(2,1)S(1)} %mlp_far2.1), channel_id=1, source_target_pairs={{0,2},{1,3},{2,0},{3,1},{4,6},{5,7},{6,4},{7,5},{8,10},{9,11},{10,... | collective-permute-start | bytes 884744 | tf_op jit(solution)/shard_map/ppermute | solution.py:33
  90.8 7.6 %collective-permute-start.29 = (bf16[64,1152]{1,0:T(8,128)(2,1)S(1)}, bf16[64,1152]{1,0:T(8,128)(2,1)S(1)}, u32[]{:S(2)}, u32[]{:S(2)}) collective-permute-start(bf16[64,1152]{1,0:T(8,128)(2,1)S(1)} %add_convert_fusion.2), channel_id=1, source_target_pairs={{0,1},{1,0},{2,3},{3,2},{4,5},{5,4},{6,7},{7,6},{8,9},{9,8},{10,11... | collective-permute-start | bytes 442376 | tf_op jit(solution)/shard_map/ppermute | solution.py:33
  92.4 6.0 %collective-permute-start.30 = (bf16[64,1152]{1,0:T(8,128)(2,1)S(1)}, bf16[64,1152]{1,0:T(8,128)(2,1)S(1)}, u32[]{:S(2)}, u32[]{:S(2)}) collective-permute-start(bf16[64,1152]{1,0:T(8,128)(2,1)S(1)} %add_convert_fusion.1), channel_id=1, source_target_pairs={{0,1},{1,0},{2,3},{3,2},{4,5},{5,4},{6,7},{7,6},{8,9},{9,8},{10,11... | collective-permute-start | bytes 442376 | tf_op jit(solution)/shard_map/ppermute | solution.py:33
  (19 other events, 111.2 us)
